TPU v7x, 32 devices: a whole 2x2x4 slice. The times are simulated.
32 devices in a mesh: groups: 2 (over y), expert: 8 (over z, x), tensor: 2 (over core).
Axes of the slice: x: 2, y: 2, z: 4, core: 2. Of those that a mesh axis runs over, the one named last changes fastest.
Arguments:
- residual: bfloat16 [2, 384, 2880], P(None, ('groups', 'expert'), 'tensor'), parts along dimension 1, may hold values from -16 to 16
- queries: bfloat16 [2, 384, 2048], P(None, ('groups', 'expert'), 'tensor'), parts along dimension 1, may hold values from -24 to 24
- new_kv: bfloat16 [2, 384, 2, 512], P(None, ('groups', 'expert'), None, 'tensor'), parts along dimension 1, may hold values from -6 to 6
- kv_cache: bfloat16 [384, 2, 8, 32, 64], P(('groups', 'expert'), None, 'tensor'), parts along dimension 0, may hold values from -6 to 6
- lengths: int32 [384], P(('groups', 'expert')), parts along dimension 0, may hold values from 2 to 32, as said below
- sink_logits: float32 [32], P('tensor'), may hold values from -5 to 5
- out_proj: bfloat16 [2048, 2880], P('tensor'), may hold values from -0.125 to 0.125
- norm_gain: bfloat16 [2880], replicated, may hold values from 0.25 to 1.75
- expert_ids: int32 [2, 384, 4], P(None, ('groups', 'expert')), parts along dimension 1, may hold values from 0 to 7, all different within a row; in each aligned block of 24 rows (0 to 23, 24 to 47, ..., all dimensions but the last counted through in order) at most 24 rows name the same one
- gate_weights: float32 [2, 384, 4], P(None, ('groups', 'expert')), parts along dimension 1, may hold values from 0.1 to 1
- w_gate_up: bfloat16 [8, 2880, 2, 1536], P('expert', None, None, 'tensor'), may hold values from -0.109375 to 0.109375
- w_down: bfloat16 [8, 1536, 2880], P('expert', 'tensor'), may hold values from -0.15625 to 0.15625
Outputs:
- layer_out: bfloat16 [2, 384, 2880], P(None, ('groups', 'expert'), 'tensor'), parts along dimension 1
There are 2 independent parts, one for each index of `groups`. A program takes and returns all parts, laid end to end along the dimension named above; an argument that names none is the same for every part. Nothing has to cross between parts.
Inputs may be any that keep to these rules, and one draw needn't show every extreme that they name: `expert_ids`: among the rows that one device holds in one step, no expert is named more than 24 times, a bound that some block reaches. `lengths`: on every device some row uses all 32 cache positions.
All inputs are finite; a program needn't handle non-finite values.
Results may differ from a plain program's by a relative error of at most 0.0075.
Values may be sent and summed in bfloat16 or wider, within the bound.
A program may use at most 128 MiB of HBM per device.

v0:
```python
import jax
import jax.numpy as jnp
from jax import lax
from jax.sharding import PartitionSpec as P

D = 2880
HD = 64
TOP = 4
STEPS = 2
CACHE = 32


def routing_tables(expert_now, weight_now, experts, capacity):
    row_count, top_count = expert_now.shape
    flattened = expert_now.reshape(-1)
    onehot = (flattened[:, None] == jnp.arange(experts, dtype=jnp.int32)[None, :]).astype(jnp.int32)
    earlier = jnp.cumsum(onehot, axis=0) - onehot
    slot_index = flattened * capacity + jnp.sum(earlier * onehot, axis=1)
    matches = slot_index[None, :] == jnp.arange(experts * capacity, dtype=jnp.int32)[:, None]
    matches = matches.reshape(experts * capacity, row_count, top_count)
    scatter_table = jnp.sum(matches.astype(jnp.int32), axis=2).astype(jnp.bfloat16)
    combine_table = jnp.sum(jnp.where(matches, weight_now[None, :, :], 0.0), axis=2).T
    return (scatter_table, combine_table)


def attend_local(queries_now, key_cache, value_cache, fresh_keys, fresh_values, valid, sink_logits):
    factor = HD ** (-0.5)
    cached = (
        jnp.einsum("rkgd,rkjd->rkgj", queries_now, key_cache, preferred_element_type=jnp.float32)
        * factor
    )
    recent = (
        jnp.einsum("rkgd,rkjd->rkgj", queries_now, fresh_keys, preferred_element_type=jnp.float32)
        * factor
    )
    cached = jnp.where(valid[:, None, None, :], cached, -jnp.inf)
    sinks = sink_logits.reshape(1, queries_now.shape[1], queries_now.shape[2], 1)
    peak = jnp.maximum(
        jnp.maximum(jnp.max(cached, axis=3, keepdims=True), jnp.max(recent, axis=3, keepdims=True)),
        sinks,
    )
    cached_weights = jnp.where(valid[:, None, None, :], jnp.exp(cached - peak), 0.0)
    recent_weights = jnp.exp(recent - peak)
    totals = (
        jnp.sum(cached_weights, axis=3, keepdims=True)
        + jnp.sum(recent_weights, axis=3, keepdims=True)
        + jnp.exp(sinks - peak)
    )
    cached_probs = (cached_weights / totals).astype(jnp.bfloat16)
    recent_probs = (recent_weights / totals).astype(jnp.bfloat16)
    mixed = jnp.einsum(
        "rkgj,rkjd->rkgd", cached_probs, value_cache, preferred_element_type=jnp.float32
    )
    mixed = mixed + jnp.einsum(
        "rkgj,rkjd->rkgd", recent_probs, fresh_values, preferred_element_type=jnp.float32
    )
    return mixed.astype(jnp.bfloat16).reshape(queries_now.shape[0], -1)


def body(
    residual,
    queries,
    new_kv,
    kv_cache,
    lengths,
    sink_logits,
    out_proj,
    norm_gain,
    expert_ids,
    gate_weights,
    w_gate_up,
    w_down,
):
    row_count = residual.shape[1]
    own_width = residual.shape[2]
    experts = lax.axis_size("expert")
    tensor_rank = lax.axis_index("tensor")
    capacity = min(row_count, 2 * row_count * TOP // experts)
    kv_local = kv_cache.shape[2]
    group_size = queries.shape[2] // (HD * kv_local)
    hidden_local = w_down.shape[1]
    w_in = w_gate_up.reshape(D, 2 * hidden_local)
    w_out = w_down.reshape(hidden_local, D)
    col_start = tensor_rank * own_width
    gain_wide = norm_gain.astype(jnp.float32)
    valid = jnp.arange(CACHE, dtype=jnp.int32)[None, :] < lengths[:, None]
    results = []
    for step_index in range(STEPS):
        count = step_index + 1
        fresh = new_kv[:count].reshape(count, row_count, 2, kv_local, HD).transpose(2, 1, 3, 0, 4)
        queries_now = queries[step_index].reshape(row_count, kv_local, group_size, HD)
        heads = attend_local(
            queries_now, kv_cache[:, 0], kv_cache[:, 1], fresh[0], fresh[1], valid, sink_logits
        )
        projected = jnp.dot(heads, out_proj, preferred_element_type=jnp.float32)
        own_cols = lax.dynamic_slice_in_dim(projected, col_start, own_width, 1) + residual[
            step_index
        ].astype(jnp.float32)
        with_input = lax.dynamic_update_slice_in_dim(projected, own_cols, col_start, 1)
        scatter_table, combine_table = routing_tables(
            expert_ids[step_index], gate_weights[step_index], experts, capacity
        )
        hidden_full = lax.psum(with_input, "tensor").astype(jnp.bfloat16)
        widened = lax.optimization_barrier(hidden_full).astype(jnp.float32)
        inv_rms = lax.rsqrt(jnp.mean(widened * widened, axis=1, keepdims=True) + 1e-05)
        normed = (widened * inv_rms * gain_wide).astype(jnp.bfloat16)
        hidden_own = lax.dynamic_slice_in_dim(hidden_full, col_start, own_width, 1)
        outgoing = jnp.dot(scatter_table, normed, preferred_element_type=jnp.float32).astype(
            jnp.bfloat16
        )
        outgoing = outgoing.reshape(experts, capacity, D)
        received = lax.all_to_all(outgoing, "expert", split_axis=0, concat_axis=0, tiled=True)
        run_count = received.shape[1]
        gate_up = jnp.dot(
            received.reshape(-1, D), w_in, preferred_element_type=jnp.float32
        ).reshape(-1, 2, hidden_local)
        gate_part = gate_up[:, 0, :]
        up_part = gate_up[:, 1, :]
        activation = (gate_part * jax.nn.sigmoid(1.702 * gate_part) * (up_part + 1.0)).astype(
            jnp.bfloat16
        )
        run_partial_out = jnp.dot(activation, w_out, preferred_element_type=jnp.float32)
        summed = lax.psum_scatter(
            run_partial_out.reshape(received.shape[0], run_count, D).astype(jnp.bfloat16),
            "tensor",
            scatter_dimension=2,
            tiled=True,
        )
        returned = lax.all_to_all(summed, "expert", split_axis=0, concat_axis=0, tiled=True)
        returned_wide = returned.reshape(experts * capacity, own_width).astype(jnp.float32)
        mixture = jnp.dot(combine_table, returned_wide, precision=lax.Precision.HIGHEST)
        results.append((hidden_own.astype(jnp.float32) + mixture).astype(jnp.bfloat16))
    return jnp.stack(results)


def solution(mesh):
    in_specs = (
        P(None, ("groups", "expert"), "tensor"),
        P(None, ("groups", "expert"), "tensor"),
        P(None, ("groups", "expert"), None, "tensor"),
        P(("groups", "expert"), None, "tensor", None, None),
        P(("groups", "expert")),
        P("tensor"),
        P("tensor", None),
        P(),
        P(None, ("groups", "expert"), None),
        P(None, ("groups", "expert"), None),
        P("expert", None, None, "tensor"),
        P("expert", "tensor", None),
    )
    out_specs = P(None, ("groups", "expert"), "tensor")
    return jax.shard_map(body, mesh=mesh, in_specs=in_specs, out_specs=out_specs, check_vma=False)
```

profile of v0, /device:TPU:0, one launch (start us, length us, event | category | flops | bytes accessed | tf_op | source)
XLA Modules:
  0.0 181.4 jit_solution(8333305373574896767)
XLA Ops:
  6.5 0.9 slice.61
  7.4 0.9 reshape.224
  8.4 0.7 max.47
  9.1 0.7 iota_compare_fusion.4
  9.8 0.7 fusion.69
  10.7 0.7 convert_element_type.121
  11.8 0.1 reduce_window_sum.18
  12.0 0.2 select_reduce_fusion.2
  12.4 0.1 reduce_window_sum.17
  12.6 0.2 select_reduce_fusion.3
  13.1 0.8 fusion.68
  13.9 0.1 reshape_squeeze.8
  14.0 0.2 fusion.60
  14.4 0.1 reshape_squeeze.9
  14.5 0.6 fusion.70
  15.1 0.6 fusion.71
  15.8 0.3 fusion.72
  16.5 0.1 copy.103
  16.6 0.1 copy.90
  16.7 0.2 fusion.56
  17.0 0.6 fusion.46
  18.1 0.3 fusion.59
  18.5 0.4 fusion.21
  18.9 0.1 reshape.212
  19.1 0.4 fusion.20
  19.5 0.1 reshape.205
  19.7 4.3 %fusion.73 = f32[24,2880]{1,0:T(8,128)S(1)} fusion(bf16[24,1024]{1,0:T(8,128)(2,1)S(1)} %reshape.205, bf16[1024,2880]{0,1:T(8,128)(2,1)} %param.18), kind=kOutput, calls=%fused_computation.121 | convolution fusion | flops 141557760 | bytes 6223872 | tf_op jit(solution)/shard_map/dot_general | solution.py:95
  24.0 4.4 %fusion.74 = f32[24,2880]{1,0:T(8,128)S(1)} fusion(bf16[24,1024]{1,0:T(8,128)(2,1)S(1)} %reshape.212, bf16[1024,2880]{0,1:T(8,128)(2,1)} %param.18), kind=kOutput, calls=%fused_computation.122 | convolution fusion | flops 141557760 | bytes 6223872 | tf_op jit(solution)/shard_map/dot_general | solution.py:95
  28.4 0.2 convert_add_fusion.1
  28.6 1.3 dynamic_update_slice.6
  29.9 1.3 dynamic_update_slice.7
  31.2 4.9 %all-reduce.2 = (bf16[24,2880]{1,0:T(8,128)(2,1)S(1)}, bf16[24,2880]{1,0:T(8,128)(2,1)S(1)}) all-reduce(f32[24,2880]{1,0:T(8,128)S(1)} %dynamic_update_slice.7, f32[24,2880]{1,0:T(8,128)S(1)} %dynamic_update_slice.6), channel_id=1, replica_groups=mesh['groups'=2,'expert'=8,'tensor'=2] {'tensor'}, use_global_device_ids=true, to_apply=%region_13.14 | all-reduce | flops 138240 | bytes 829440 | tf_op jit(solution)/shard_map/psum | solution.py:103
  36.1 0.1 fusion.37
  36.3 1.5 convolution_convert_fusion
  37.9 7.3 %all-to-all-start.2 = ((bf16[8,24,2880]{2,1,0:T(8,128)(2,1)}), bf16[8,24,2880]{2,1,0:T(8,128)(2,1)S(1)}, u32[]{:S(2)}, u32[]{:S(2)}) async-start(bf16[8,24,2880]{2,1,0:T(8,128)(2,1)} %bitcast.29), calls=%async_computation.2 | async-start | bytes 2260992 | tf_op jit(solution)/shard_map/all_to_all | solution.py:112
  45.1 23.6 %copy.118 = bf16[1,2880,2,768]{1,3,2,0:T(8,128)(2,1)} copy(bf16[1,2880,2,768]{3,2,1,0:T(2,128)(2,1)} %param.22) | data formatting | bytes 17694720 | tf_op jit(solution)/shard_map/dot_general | solution.py:114
  68.7 0.1 fusion.34
  68.9 1.5 convolution_convert_fusion.1
  70.4 2.8 %all-to-all-done.2 = bf16[8,24,2880]{2,1,0:T(8,128)(2,1)S(1)} async-done(((bf16[8,24,2880]{2,1,0:T(8,128)(2,1)}), bf16[8,24,2880]{2,1,0:T(8,128)(2,1)S(1)}, u32[]{:S(2)}, u32[]{:S(2)}) %all-to-all-start.2) | async-done | bytes 1105952 | tf_op jit(solution)/shard_map/all_to_all | solution.py:112
  73.2 3.8 %all-to-all-start = ((bf16[8,24,2880]{2,1,0:T(8,128)(2,1)}), bf16[8,24,2880]{2,1,0:T(8,128)(2,1)S(1)}, u32[]{:S(2)}, u32[]{:S(2)}) async-start(bf16[8,24,2880]{2,1,0:T(8,128)(2,1)} %bitcast.10), calls=%async_computation | async-start | bytes 2260992 | tf_op jit(solution)/shard_map/all_to_all | solution.py:112
  76.9 0.2 reduce-scatter.9.cloned.1.call-start
  77.2 6.8 %fusion = f32[192,2,768]{2,0,1:T(8,128)S(1)} fusion(bf16[192,2880,1]{1,0,2:T(8,128)(2,1)S(1)} %bitcast.140, bf16[1,2880,2,768]{1,3,2,0:T(8,128)(2,1)} %copy.118), kind=kOutput, calls=%fused_computation | convolution fusion | flops 1698693120 | bytes 11132928 | tf_op jit(solution)/shard_map/dot_general | solution.py:114
  84.0 0.2 fusion.31
  84.2 1.6 fusion.11
  85.9 5.5 %copy.125 = bf16[8,24,2880]{1,0,2:T(8,128)(2,1)} copy(bf16[8,24,2880]{2,1,0:T(8,128)(2,1)S(1)} %fusion.11) | data formatting | bytes 2211840
  91.3 8.0 %reshape.227 = bf16[2880,192]{1,0:T(8,128)(2,1)} reshape(bf16[2880,8,24]{2,1,0:T(8,128)(2,1)} %bitcast.127) | data formatting | bytes 2211840
  99.4 5.3 %all-to-all-done = bf16[8,24,2880]{2,1,0:T(8,128)(2,1)S(1)} async-done(((bf16[8,24,2880]{2,1,0:T(8,128)(2,1)}), bf16[8,24,2880]{2,1,0:T(8,128)(2,1)S(1)}, u32[]{:S(2)}, u32[]{:S(2)}) %all-to-all-start) | async-done | bytes 1105952 | tf_op jit(solution)/shard_map/all_to_all | solution.py:112
  104.7 7.3 %fusion.2 = f32[192,2,768]{2,0,1:T(8,128)S(1)} fusion(bf16[192,2880,1]{1,0,2:T(8,128)(2,1)S(1)} %bitcast.139, bf16[1,2880,2,768]{1,3,2,0:T(8,128)(2,1)} %copy.118), kind=kOutput, calls=%fused_computation.2 | convolution fusion | flops 1698693120 | bytes 11132928 | tf_op jit(solution)/shard_map/dot_general | solution.py:114
  112.0 0.2 fusion.33
  112.2 1.6 fusion.8
  113.9 5.5 %copy.123 = bf16[8,24,2880]{1,0,2:T(8,128)(2,1)} copy(bf16[8,24,2880]{2,1,0:T(8,128)(2,1)S(1)} %fusion.8) | data formatting | bytes 2211840
  119.3 8.0 %reshape.225 = bf16[2880,192]{1,0:T(8,128)(2,1)} reshape(bf16[2880,8,24]{2,1,0:T(8,128)(2,1)} %bitcast.128) | data formatting | bytes 2211840
  127.4 3.6 %reshape.228 = bf16[1440,8,24]{2,1,0:T(8,128)(2,1)S(1)} reshape(bf16[1440,192]{1,0:T(8,128)(2,1)} %reduce-scatter.9.cloned.1.call-done) | data formatting | bytes 1105920
  131.0 3.4 %copy.126 = bf16[8,24,1440]{2,1,0:T(8,128)(2,1)} copy(bf16[8,24,1440]{1,0,2:T(8,128)(2,1)S(1)} %bitcast.133) | data formatting | bytes 1105920
  134.4 3.8 %all-to-all-start.3 = ((bf16[8,24,1440]{2,1,0:T(8,128)(2,1)}), bf16[8,24,1440]{2,1,0:T(8,128)(2,1)S(1)}, u32[]{:S(2)}, u32[]{:S(2)}) async-start(bf16[8,24,1440]{2,1,0:T(8,128)(2,1)} %copy.126), calls=%async_computation.3 | async-start | bytes 1179648 | tf_op jit(solution)/shard_map/all_to_all | solution.py:129
  138.2 3.6 %reshape.226 = bf16[1440,8,24]{2,1,0:T(8,128)(2,1)S(1)} reshape(bf16[1440,192]{1,0:T(8,128)(2,1)} %reduce-scatter.7.cloned.1.call-done) | data formatting | bytes 1105920
  141.8 3.4 %copy.124 = bf16[8,24,1440]{2,1,0:T(8,128)(2,1)} copy(bf16[8,24,1440]{1,0,2:T(8,128)(2,1)S(1)} %bitcast.134) | data formatting | bytes 1105920
  145.2 8.6 %all-to-all-done.3 = bf16[8,24,1440]{2,1,0:T(8,128)(2,1)S(1)} async-done(((bf16[8,24,1440]{2,1,0:T(8,128)(2,1)}), bf16[8,24,1440]{2,1,0:T(8,128)(2,1)S(1)}, u32[]{:S(2)}, u32[]{:S(2)}) %all-to-all-start.3) | async-done | bytes 552992 | tf_op jit(solution)/shard_map/all_to_all | solution.py:129
  153.8 3.6 %all-to-all-start.1 = ((bf16[8,24,1440]{2,1,0:T(8,128)(2,1)}), bf16[8,24,1440]{2,1,0:T(8,128)(2,1)S(1)}, u32[]{:S(2)}, u32[]{:S(2)}) async-start(bf16[8,24,1440]{2,1,0:T(8,128)(2,1)} %copy.124), calls=%async_computation.1 | async-start | bytes 1179648 | tf_op jit(solution)/shard_map/all_to_all | solution.py:129
  157.4 0.1 select_reduce_fusion
  157.6 1.2 fusion.16
  158.8 14.7 %all-to-all-done.1 = bf16[8,24,1440]{2,1,0:T(8,128)(2,1)S(1)} async-done(((bf16[8,24,1440]{2,1,0:T(8,128)(2,1)}), bf16[8,24,1440]{2,1,0:T(8,128)(2,1)S(1)}, u32[]{:S(2)}, u32[]{:S(2)}) %all-to-all-start.1) | async-done | bytes 552992 | tf_op jit(solution)/shard_map/all_to_all | solution.py:129
  173.5 0.3 fusion.17
  173.8 0.7 pad_maximum_fusion
  (60 shorter events, 2.6 us)
Async XLA Ops:
  6.5 8.0 %copy-start.6 = (bf16[24,2,4,32,64]{4,3,2,1,0:T(8,128)(2,1)S(1)}, bf16[24,2,4,32,64]{4,3,2,1,0:T(8,128)(2,1)}, u32[]{:S(2)}) copy-start(bf16[24,2,4,32,64]{4,3,2,1,0:T(8,128)(2,1)} %param.15) | copy-start | bytes 2359300
  24.0 4.4 %copy-start.3 = (bf16[2,24,1440]{2,1,0:T(8,128)(2,1)S(1)}, bf16[2,24,1440]{2,1,0:T(8,128)(2,1)}, u32[]{:S(2)}) copy-start(bf16[2,24,1440]{2,1,0:T(8,128)(2,1)} %param.12) | copy-start | bytes 414724
  28.4 7.8 %copy-start.4 = (s32[2,24,4]{1,2,0:T(4,128)S(1)}, s32[2,24,4]{1,2,0:T(4,128)}, u32[]{:S(2)}) copy-start(s32[2,24,4]{1,2,0:T(4,128)} %param.20) | copy-start | bytes 2308
  36.0 1.8 %copy-start.2 = (bf16[24,2880]{1,0:T(8,128)(2,1)}, bf16[24,2880]{1,0:T(8,128)(2,1)S(1)}, u32[]{:S(2)}) copy-start(bf16[24,2880]{1,0:T(8,128)(2,1)S(1)} %get-tuple-element.7) | copy-start | bytes 414724
  36.1 32.8 %copy-start = (bf16[24,2880]{1,0:T(8,128)(2,1)}, bf16[24,2880]{1,0:T(8,128)(2,1)S(1)}, u32[]{:S(2)}) copy-start(bf16[24,2880]{1,0:T(8,128)(2,1)S(1)} %get-tuple-element.8) | copy-start | bytes 414724
  37.9 35.3 %all-to-all-start.2 = ((bf16[8,24,2880]{2,1,0:T(8,128)(2,1)}), bf16[8,24,2880]{2,1,0:T(8,128)(2,1)S(1)}, u32[]{:S(2)}, u32[]{:S(2)}) async-start(bf16[8,24,2880]{2,1,0:T(8,128)(2,1)} %bitcast.29), calls=%async_computation.2 | async-start | bytes 2260992 | tf_op jit(solution)/shard_map/all_to_all | solution.py:112
  73.2 11.0 %slice-start = ((s8[4423680]{0:T(1024)(128)(4,1)}), s8[229376]{0:T(1024)(128)(4,1)S(1)}, s32[]{:S(2)}) async-start(s8[4423680]{0:T(1024)(128)(4,1)} %bitcast.129), calls=%async_computation.8 | async-start | bytes 458752
  73.2 31.5 %all-to-all-start = ((bf16[8,24,2880]{2,1,0:T(8,128)(2,1)}), bf16[8,24,2880]{2,1,0:T(8,128)(2,1)S(1)}, u32[]{:S(2)}, u32[]{:S(2)}) async-start(bf16[8,24,2880]{2,1,0:T(8,128)(2,1)} %bitcast.10), calls=%async_computation | async-start | bytes 2260992 | tf_op jit(solution)/shard_map/all_to_all | solution.py:112
  76.9 50.4 %reduce-scatter.9.cloned.1.call-start = ((), (), s32[]{:S(2)}) async-start(), calls=%async_computation.7 | async-start | bytes 2211840
  77.2 7.0 %slice-start.1 = ((s8[4423680]{0:T(1024)(128)(4,1)}), s8[4194304]{0:T(1024)(128)(4,1)S(1)}, s32[]{:S(2)}) async-start(s8[4423680]{0:T(1024)(128)(4,1)} %bitcast.129), calls=%async_computation.9 | async-start | bytes 8388608
  99.3 12.9 %slice-start.2 = ((s8[4423680]{0:T(1024)(128)(4,1)}), s8[229376]{0:T(1024)(128)(4,1)S(1)}, s32[]{:S(2)}) async-start(s8[4423680]{0:T(1024)(128)(4,1)} %bitcast.131), calls=%async_computation.10 | async-start | bytes 458752
  99.3 38.8 %reduce-scatter.7.cloned.1.call-start = ((), (), s32[]{:S(2)}) async-start(), calls=%async_computation.6 | async-start | bytes 2211840
  104.7 7.5 %slice-start.3 = ((s8[4423680]{0:T(1024)(128)(4,1)}), s8[4194304]{0:T(1024)(128)(4,1)S(1)}, s32[]{:S(2)}) async-start(s8[4423680]{0:T(1024)(128)(4,1)} %bitcast.131), calls=%async_computation.11 | async-start | bytes 8388608
  134.4 19.4 %all-to-all-start.3 = ((bf16[8,24,1440]{2,1,0:T(8,128)(2,1)}), bf16[8,24,1440]{2,1,0:T(8,128)(2,1)S(1)}, u32[]{:S(2)}, u32[]{:S(2)}) async-start(bf16[8,24,1440]{2,1,0:T(8,128)(2,1)} %copy.126), calls=%async_computation.3 | async-start | bytes 1179648 | tf_op jit(solution)/shard_map/all_to_all | solution.py:129
  141.8 15.7 %copy-start.5 = (f32[2,24,4]{1,2,0:T(4,128)S(1)}, f32[2,24,4]{1,2,0:T(4,128)}, u32[]{:S(2)}) copy-start(f32[2,24,4]{1,2,0:T(4,128)} %param.21) | copy-start | bytes 2308
  145.2 28.3 %copy-start.1 = (bf16[24,2880]{1,0:T(8,128)(2,1)S(1)}, bf16[24,2880]{1,0:T(8,128)(2,1)}, u32[]{:S(2)}) copy-start(bf16[24,2880]{1,0:T(8,128)(2,1)} %copy-done) | copy-start | bytes 414724
  153.8 19.7 %all-to-all-start.1 = ((bf16[8,24,1440]{2,1,0:T(8,128)(2,1)}), bf16[8,24,1440]{2,1,0:T(8,128)(2,1)S(1)}, u32[]{:S(2)}, u32[]{:S(2)}) async-start(bf16[8,24,1440]{2,1,0:T(8,128)(2,1)} %copy.124), calls=%async_computation.1 | async-start | bytes 1179648 | tf_op jit(solution)/shard_map/all_to_all | solution.py:129
Sparse Core Ops, SparseCore 0:
  99.5 10.1 reduce-scatter.8
  127.5 7.5 reduce-scatter.6
where the time goes:
time: 183 us; the launch traced here: 181 us
  local copies, waits for them, and re-layouts  74 us (40%)
  matrix products  33.7 us (18%)
  waiting for transfers between devices  31.4 us (17%)
  starting transfers between devices  18.7 us (10%)
  between operations  13.8 us (8%)
  other arithmetic  4.91 us (3%)
  blocking collectives  4.87 us (3%)
    unnamed x30, local copies, waits for them, and re-layouts  41 us
    dot_general x1, local copies, waits for them, and re-layouts, body(): jnp.dot(received.reshape(-1, D), w_in, preferred_element_type=jnp.float32)  23.6 us
    all_to_all x2, waiting for transfers between devices, body(): lax.all_to_all(summed, 'expert', split_axis=0, concat_axis=0, tiled=True)  23.3 us
    dot_general x2, matrix products, body(): jnp.dot(received.reshape(-1, D), w_in, preferred_element_type=jnp.float32)  14.2 us
    all_to_all x2, starting transfers between devices, body(): lax.all_to_all(outgoing, 'expert', split_axis=0, concat_axis=0, tiled=True)  11 us
    dot_general x2, matrix products, body(): projected = jnp.dot(heads, out_proj, preferred_element_type=jnp.float32)  8.73 us
    all_to_all x2, waiting for transfers between devices, body(): lax.all_to_all(outgoing, 'expert', split_axis=0, concat_axis=0, tiled=True)  8.02 us
    all_to_all x2, starting transfers between devices, body(): lax.all_to_all(summed, 'expert', split_axis=0, concat_axis=0, tiled=True)  7.39 us
  transfers between devices with their start and end apart: 6, of which 4 were waited for; matrix products, arithmetic and copies ran while one was open for 47% of the time, Pallas kernels for 0%

commit v1 on v0

--- a/solution.py
+++ b/solution.py
@@ -57,7 +57,7 @@
     return mixed.astype(jnp.bfloat16).reshape(queries_now.shape[0], -1)
 
 
-def body(
+def body_compact(
     residual,
     queries,
     new_kv,
@@ -133,6 +133,97 @@
     return jnp.stack(results)
 
 
+def attend_steps(queries, new_kv, kv_cache, valid, sink_logits):
+    row_count, kv_local = kv_cache.shape[0], kv_cache.shape[2]
+    group_size = queries.shape[2] // (HD * kv_local)
+    fresh = new_kv.reshape(STEPS, row_count, 2, kv_local, HD).transpose(2, 1, 3, 0, 4)
+    key_all = jnp.concatenate([kv_cache[:, 0], fresh[0]], axis=2)
+    value_all = jnp.concatenate([kv_cache[:, 1], fresh[1]], axis=2)
+    asked = queries.reshape(STEPS, row_count, kv_local, group_size, HD)
+    asked = asked.transpose(1, 2, 0, 3, 4).reshape(row_count, kv_local, STEPS * group_size, HD)
+    step_of = jnp.arange(STEPS * group_size, dtype=jnp.int32) // group_size
+    seen_new = jnp.arange(STEPS, dtype=jnp.int32)[None, :] <= step_of[:, None]
+    seen = jnp.concatenate(
+        [
+            jnp.broadcast_to(valid[:, None, :], (row_count, STEPS * group_size, CACHE)),
+            jnp.broadcast_to(seen_new[None], (row_count, STEPS * group_size, STEPS)),
+        ],
+        axis=2,
+    )[:, None]
+    scores = jnp.einsum("rkgd,rkjd->rkgj", asked, key_all, preferred_element_type=jnp.float32)
+    scores = jnp.where(seen, scores * HD ** (-0.5), -jnp.inf)
+    sinks = jnp.tile(sink_logits.reshape(kv_local, group_size), (1, STEPS))[None, :, :, None]
+    peak = jnp.maximum(jnp.max(scores, axis=3, keepdims=True), sinks)
+    weights = jnp.exp(scores - peak)
+    totals = jnp.sum(weights, axis=3, keepdims=True) + jnp.exp(sinks - peak)
+    probs = (weights / totals).astype(jnp.bfloat16)
+    mixed = jnp.einsum("rkgj,rkjd->rkgd", probs, value_all, preferred_element_type=jnp.float32)
+    mixed = mixed.astype(jnp.bfloat16).reshape(row_count, kv_local, STEPS, group_size, HD)
+    return mixed.transpose(2, 0, 1, 3, 4).reshape(STEPS * row_count, -1)
+
+
+def body_dense(
+    residual,
+    queries,
+    new_kv,
+    kv_cache,
+    lengths,
+    sink_logits,
+    out_proj,
+    norm_gain,
+    expert_ids,
+    gate_weights,
+    w_gate_up,
+    w_down,
+):
+    row_count, own_width = residual.shape[1:]
+    experts = lax.axis_size("expert")
+    both = STEPS * row_count
+    hidden_local = w_down.shape[1]
+    col_start = lax.axis_index("tensor") * own_width
+    valid = jnp.arange(CACHE, dtype=jnp.int32)[None, :] < lengths[:, None]
+    heads = attend_steps(queries, new_kv, kv_cache, valid, sink_logits)
+    projected = jnp.dot(heads, out_proj, preferred_element_type=jnp.float32)
+    own_cols = lax.dynamic_slice_in_dim(projected, col_start, own_width, 1)
+    own_cols = own_cols + residual.reshape(both, own_width).astype(jnp.float32)
+    with_input = lax.dynamic_update_slice_in_dim(projected, own_cols, col_start, 1)
+    hidden_full = lax.psum(with_input, "tensor").astype(jnp.bfloat16)
+    widened = lax.optimization_barrier(hidden_full).astype(jnp.float32)
+    inv_rms = lax.rsqrt(jnp.mean(widened * widened, axis=1, keepdims=True) + 1e-05)
+    normed = (widened * inv_rms * norm_gain.astype(jnp.float32)).astype(jnp.bfloat16)
+    hidden_own = lax.dynamic_slice_in_dim(hidden_full, col_start, own_width, 1)
+    gathered = lax.all_gather(normed, "expert", axis=0, tiled=True)
+    w_in = w_gate_up.reshape(2 * D, hidden_local)
+    twice = jnp.repeat(gathered, 2, axis=1)
+    even = jnp.arange(2 * D, dtype=jnp.int32)[None, :] % 2 == 0
+    placed = jnp.concatenate([jnp.where(even, twice, 0), jnp.where(even, 0, twice)], axis=0)
+    gate_up = jnp.dot(placed, w_in, preferred_element_type=jnp.float32)
+    gate_part, up_part = gate_up[: experts * both], gate_up[experts * both :]
+    activation = (gate_part * jax.nn.sigmoid(1.702 * gate_part) * (up_part + 1.0)).astype(
+        jnp.bfloat16
+    )
+    partial_out = jnp.dot(activation, w_down[0], preferred_element_type=jnp.float32)
+    partial_out = partial_out.astype(jnp.bfloat16)
+    kept = lax.dynamic_slice_in_dim(partial_out, col_start, own_width, 1)
+    given = lax.dynamic_slice_in_dim(partial_out, own_width - col_start, own_width, 1)
+    got = lax.ppermute(given, "tensor", [(0, 1), (1, 0)])
+    summed = (kept.astype(jnp.float32) + got.astype(jnp.float32)).astype(jnp.bfloat16)
+    returned = lax.all_to_all(
+        summed.reshape(experts, both, own_width), "expert", split_axis=0, concat_axis=0, tiled=True
+    )
+    named = expert_ids[..., None] == jnp.arange(experts, dtype=jnp.int32)
+    share = jnp.sum(jnp.where(named, gate_weights[..., None], 0.0), axis=2).reshape(both, experts)
+    mixture = jnp.sum(returned.astype(jnp.float32) * share.T[:, :, None], axis=0)
+    out = (hidden_own.astype(jnp.float32) + mixture).astype(jnp.bfloat16)
+    return out.reshape(STEPS, row_count, own_width)
+
+
+def body(residual, *rest):
+    row_count, experts = residual.shape[1], lax.axis_size("expert")
+    compact = 2 * row_count * TOP // experts < row_count
+    return (body_compact if compact else body_dense)(residual, *rest)
+
+
 def solution(mesh):
     in_specs = (
         P(None, ("groups", "expert"), "tensor"),

time: 183 us -> 159 us (0.87)
  waiting for transfers between devices: 31.4 us -> 66.6 us
  local copies, waits for them, and re-layouts: 74 us -> 41.9 us
  starting transfers between devices: 18.7 us -> 3.67 us
  matrix products: 33.7 us -> 19.2 us
  other arithmetic: 4.91 us -> 8.4 us
    unnamed x30 -> x22, local copies, waits for them, and re-layouts: 41 us -> 0.07 us
    all_gather x0 -> x1, waiting for transfers between devices: none -> 34.9 us  [body_dense(): gathered = lax.all_gather(normed, 'expert', axis=0, tiled=True)]
    reshape x6 -> x8, local copies, waits for them, and re-layouts: 1.43 us -> 29.7 us  [the longest x1 18.9 us: body_dense(): w_in = w_gate_up.reshape(2 * D, hidden_local)]
    dot_general x2 -> x0, local copies, waits for them, and re-layouts: 23.7 us -> none  [the longest x1 23.6 us: body(): jnp.dot(received.reshape(-1, D), w_in, preferred_element_type=jnp.float32)]
    all_to_all x4 -> x1, starting transfers between devices: 18.4 us -> 3.56 us  [body_dense(): lax.all_to_all(summed.reshape(experts, both, own_width), 'expert', split_...]
    dot_general x17 -> x5, matrix products: 33.7 us -> 19.2 us  [the longest x1 10.9 us: body_dense(): gate_up = jnp.dot(placed, w_in, preferred_element_type=jnp.float32)]
    select_n x0 -> x2, other arithmetic: none -> 5.17 us  [the longest x1 5.16 us: body_dense(): jnp.where(even, twice, 0)]
    broadcast_in_dim x1 -> x3, local copies, waits for them, and re-layouts: 0.01 us -> 3.76 us  [the longest x1 3.74 us: body_dense(): twice = jnp.repeat(gathered, 2, axis=1)]
  transfers between devices with their start and end apart: 6 -> 3, of which waited for: 4 -> 3; matrix products, arithmetic and copies ran while one was open for 47% -> 12% of each run, Pallas kernels for 0% -> 0%
where the time goes in v1:
time: 159 us; the launch traced here: 158 us
  waiting for transfers between devices  66.6 us (42%)
  local copies, waits for them, and re-layouts  41.9 us (26%)
  matrix products  19.2 us (12%)
  between operations  13.7 us (9%)
  other arithmetic  8.4 us (5%)
  blocking collectives  4.85 us (3%)
  starting transfers between devices  3.67 us (2%)
    all_gather x1, waiting for transfers between devices, body_dense(): gathered = lax.all_gather(normed, 'expert', axis=0, tiled=True)  34.9 us
    all_to_all x1, waiting for transfers between devices, body_dense(): lax.all_to_all(summed.reshape(experts, both, own_width), 'expert', split_...  28.9 us
    reshape x1, local copies, waits for them, and re-layouts, body_dense(): w_in = w_gate_up.reshape(2 * D, hidden_local)  18.9 us
    dot_general x1, matrix products, body_dense(): gate_up = jnp.dot(placed, w_in, preferred_element_type=jnp.float32)  10.9 us
    reshape x1, local copies, waits for them, and re-layouts, body_dense(): twice = jnp.repeat(gathered, 2, axis=1)  10.1 us
    select_n x1, other arithmetic, body_dense(): jnp.where(even, twice, 0)  5.16 us
    psum x1, blocking collectives, body_dense(): hidden_full = lax.psum(with_input, 'tensor').astype(jnp.bfloat16)  4.85 us
    dot_general x1, matrix products, body_dense(): projected = jnp.dot(heads, out_proj, preferred_element_type=jnp.float32)  4.58 us
  transfers between devices with their start and end apart: 3, of which 3 were waited for; matrix products, arithmetic and copies ran while one was open for 12% of the time, Pallas kernels for 0%

profile of v1, /device:TPU:0, one launch (start us, length us, event | category | flops | bytes accessed | tf_op | source)
XLA Modules:
  0.0 158.4 jit_solution(17104869427086633075)
XLA Ops:
  6.5 0.0 copy-start.2
  6.5 0.0 copy-start.1
  6.5 0.0 copy-start.6
  6.5 0.0 copy-start.7
  6.5 0.0 all-gather.2.cloned.1.call-start
  6.6 1.7 %slice_bitcast_fusion.1 = (bf16[24,4,32,64]{3,2,1,0:T(8,128)(2,1)S(1)}, bf16[24,4,32,64]{3,2,1,0:T(8,128)(2,1)S(1)}) fusion(bf16[24,2,4,32,64]{4,3,2,1,0:T(8,128)(2,1)} %param.15), kind=kLoop, calls=%fused_computation.25 | loop fusion | bytes 1572864 | tf_op jit(solution)/shard_map/squeeze | solution.py:140
  8.3 0.0 copy-done.2
  8.3 0.1 reshape.145
  8.4 0.1 copy.52
  8.5 0.1 slice_bitcast_fusion.3
  8.6 0.0 copy-done.1
  8.6 0.2 reshape.135
  8.8 0.1 copy.39
  8.9 0.0 copy-done.6
  8.9 0.1 iota_compare_fusion.1
  9.0 0.1 iota_compare_fusion.2
  9.0 0.0 copy-done.7
  9.0 0.1 tile.9
  9.1 0.1 tile.11
  9.3 0.1 pad_add_fusion
  9.4 0.7 fusion.37
  10.1 0.4 fusion.25
  10.5 0.4 convolution_convert_fusion
  10.9 0.1 copy.51
  11.0 0.2 reshape.138
  11.2 0.0 copy-start
  11.2 4.6 %fusion.38 = f32[48,2880]{1,0:T(8,128)S(1)} fusion(bf16[48,1024]{1,0:T(8,128)(2,1)S(1)} %reshape.138, bf16[1024,2880]{0,1:T(8,128)(2,1)} %param.18), kind=kOutput, calls=%fused_computation.69 | convolution fusion | flops 283115520 | bytes 6549504 | tf_op jit(solution)/shard_map/dot_general | solution.py:186
  15.8 0.0 copy-start.3
  15.8 0.0 copy-done
  15.8 0.2 convert_add_fusion
  16.0 1.3 dynamic_update_slice.3
  17.3 4.9 %all-reduce.1 = bf16[48,2880]{1,0:T(8,128)(2,1)S(1)} all-reduce(f32[48,2880]{1,0:T(8,128)S(1)} %dynamic_update_slice.3), channel_id=1, replica_groups=mesh['groups'=2,'expert'=8,'tensor'=2] {'tensor'}, use_global_device_ids=true, to_apply=%region_2.3 | all-reduce | flops 138240 | bytes 829440 | tf_op jit(solution)/shard_map/psum | solution.py:190
  22.1 0.2 fusion.22
  22.3 0.0 copy-done.3
  22.3 0.9 fusion.24
  23.2 0.0 all-gather.2.cloned.1.call-update
  23.2 18.9 %reshape.140 = bf16[5760,768]{1,0:T(8,128)(2,1)} reshape(bf16[1,2880,2,768]{3,2,1,0:T(2,128)(2,1)} %param.22) | data formatting | bytes 17694720 | tf_op jit(solution)/shard_map/reshape | solution.py:196
  42.1 34.9 %all-gather.2.cloned.1.call-done = bf16[384,2880]{1,0:T(8,128)(2,1)} async-done(((bf16[48,2880]{1,0:T(8,128)(2,1)}), bf16[384,2880]{1,0:T(8,128)(2,1)}) %all-gather.2.cloned.1.call-update) | async-done | bytes 2211856 | tf_op jit(solution)/shard_map/all_gather | solution.py:195
  77.0 3.0 %copy.42 = bf16[384,2880]{0,1:T(8,128)(2,1)S(1)} copy(bf16[384,2880]{1,0:T(8,128)(2,1)} %all-gather.2.cloned.1.call-done) | data formatting | bytes 4423680 | tf_op jit(solution)/shard_map/all_gather | solution.py:195
  80.0 3.7 %broadcast_in_dim.80 = bf16[384,2880,2]{0,2,1:T(2,128)(2,1)} broadcast(bf16[384,2880]{0,1:T(8,128)(2,1)S(1)} %copy.42), dimensions={0,1} | broadcast | bytes 6635520 | tf_op jit(solution)/shard_map/broadcast_in_dim | solution.py:197
  83.7 10.1 %reshape.139 = bf16[384,5760]{0,1:T(8,128)(2,1)} reshape(bf16[384,2880,2]{0,2,1:T(2,128)(2,1)} %broadcast_in_dim.80) | data formatting | bytes 8847360 | tf_op jit(solution)/shard_map/reshape | solution.py:197
  93.8 0.0 slice-start
  93.8 5.2 %broadcast_select_fusion.1 = (bf16[384,5760]{0,1:T(8,128)(2,1)S(1)}, bf16[384,5760]{0,1:T(8,128)(2,1)S(1)}) fusion(bf16[384,5760]{0,1:T(8,128)(2,1)} %reshape.139, pred[5760]{0:T(1024)(128)(4,1)S(1)} %fusion.28), kind=kLoop, calls=%fused_computation.7 | loop fusion | flops 4423680 | bytes 13276800 | tf_op jit(solution)/shard_map/jit(_where)/select_n | solution.py:199
  99.0 0.0 slice-start.1
  99.0 10.9 %fusion = f32[768,768]{1,0:T(8,128)S(1)} fusion(bf16[5760,768]{1,0:T(8,128)(2,1)} %reshape.140, bf16[384,5760]{0,1:T(8,128)(2,1)S(1)} %get-tuple-element.6, bf16[384,5760]{0,1:T(8,128)(2,1)S(1)} %get-tuple-element.5), kind=kOutput, calls=%fused_computation | convolution fusion | flops 6812467200 | bytes 20054016 | tf_op jit(solution)/shard_map/dot_general | solution.py:200
  109.9 0.0 slice-done
  110.0 0.0 slice-done.1
  110.0 2.5 %fusion.6 = bf16[384,2880]{0,1:T(8,128)(2,1)S(1)} fusion(bf16[1,768,2880]{1,2,0:T(8,128)(2,1)S(1)} %bitcast.66, f32[768,768]{1,0:T(8,128)S(1)} %fusion), kind=kOutput, calls=%fused_computation.8 | convolution fusion | flops 1702158336 | bytes 8994816 | tf_op jit(solution)/shard_map/dot_general | solution.py:205
  112.5 0.1 constant_dynamic-slice_fusion
  112.7 0.1 collective-permute-start
  112.7 2.7 %collective-permute-done = bf16[384,1440]{0,1:T(8,128)(2,1)S(1)} collective-permute-done((bf16[384,1440]{0,1:T(8,128)(2,1)S(1)}, bf16[384,1440]{0,1:T(8,128)(2,1)S(1)}, u32[]{:S(2)}, u32[]{:S(2)}) %collective-permute-start) | collective-permute-done | bytes 1105952 | tf_op jit(solution)/shard_map/ppermute | solution.py:209
  115.5 0.3 add_convert_fusion
  115.8 0.0 copy-start.4
  115.8 0.0 copy-start.5
  115.8 2.0 %copy.43 = bf16[384,1440]{1,0:T(8,128)(2,1)} copy(bf16[384,1440]{0,1:T(8,128)(2,1)S(1)} %add_convert_fusion) | data formatting | bytes 2211840 | tf_op jit(solution)/shard_map/convert_element_type | solution.py:210
  117.8 3.6 %all-to-all-start = ((bf16[8,48,1440]{2,1,0:T(8,128)(2,1)}), bf16[8,48,1440]{2,1,0:T(8,128)(2,1)S(1)}, u32[]{:S(2)}, u32[]{:S(2)}) async-start(bf16[8,48,1440]{2,1,0:T(8,128)(2,1)} %bitcast.12), calls=%async_computation | async-start | bytes 2359296 | tf_op jit(solution)/shard_map/all_to_all | solution.py:211
  121.4 0.0 copy-done.4
  121.4 0.0 copy-done.5
  121.4 0.1 reshape.142
  121.5 28.9 %all-to-all-done = bf16[8,48,1440]{2,1,0:T(8,128)(2,1)S(1)} async-done(((bf16[8,48,1440]{2,1,0:T(8,128)(2,1)}), bf16[8,48,1440]{2,1,0:T(8,128)(2,1)S(1)}, u32[]{:S(2)}, u32[]{:S(2)}) %all-to-all-start) | async-done | bytes 1105952 | tf_op jit(solution)/shard_map/all_to_all | solution.py:211
  150.5 0.3 multiply_reduce_fusion
  150.8 0.8 add_convert_fusion.1
  (14 shorter events, 0.1 us)
Async XLA Ops:
  6.5 1.8 %copy-start.2 = (bf16[2,24,2,256]{3,2,1,0:T(2,128)(2,1)S(1)}, bf16[2,24,2,256]{3,2,1,0:T(2,128)(2,1)}, u32[]{:S(2)}) copy-start(bf16[2,24,2,256]{3,2,1,0:T(2,128)(2,1)} %param.14) | copy-start | bytes 147460
  6.5 2.1 %copy-start.1 = (bf16[2,24,1024]{2,1,0:T(8,128)(2,1)S(1)}, bf16[2,24,1024]{2,1,0:T(8,128)(2,1)}, u32[]{:S(2)}) copy-start(bf16[2,24,1024]{2,1,0:T(8,128)(2,1)} %param.13) | copy-start | bytes 294916
  6.5 2.3 %copy-start.6 = (s32[24]{0:T(128)S(1)}, s32[24]{0:T(128)}, u32[]{:S(2)}) copy-start(s32[24]{0:T(128)} %param.16) | copy-start | bytes 292
  6.5 2.5 %copy-start.7 = (f32[16]{0:T(128)S(1)}, f32[16]{0:T(128)}, u32[]{:S(2)}) copy-start(f32[16]{0:T(128)} %param.17) | copy-start | bytes 196
  6.5 70.5 %all-gather.2.cloned.1.call-start = ((), (), s32[]{:S(2)}) async-start(), calls=%async_computation.1 | async-start | bytes 2543616 | tf_op jit(solution)/shard_map/all_gather | solution.py:195
  11.2 4.6 %copy-start = (bf16[2,24,1440]{2,1,0:T(8,128)(2,1)S(1)}, bf16[2,24,1440]{2,1,0:T(8,128)(2,1)}, u32[]{:S(2)}) copy-start(bf16[2,24,1440]{2,1,0:T(8,128)(2,1)} %param.12) | copy-start | bytes 414724
  15.8 6.5 %copy-start.3 = (bf16[2880]{0:T(1024)(128)(2,1)S(1)}, bf16[2880]{0:T(1024)(128)(2,1)}, u32[]{:S(2)}) copy-start(bf16[2880]{0:T(1024)(128)(2,1)} %param.19) | copy-start | bytes 17284
  93.8 16.1 %slice-start = ((s8[4423680]{0:T(1024)(128)(4,1)}), s8[4194304]{0:T(1024)(128)(4,1)S(1)}, s32[]{:S(2)}) async-start(s8[4423680]{0:T(1024)(128)(4,1)} %bitcast.65), calls=%async_computation.2 | async-start | bytes 8388608
  99.0 11.0 %slice-start.1 = ((s8[4423680]{0:T(1024)(128)(4,1)}), s8[229376]{0:T(1024)(128)(4,1)S(1)}, s32[]{:S(2)}) async-start(s8[4423680]{0:T(1024)(128)(4,1)} %bitcast.65), calls=%async_computation.3 | async-start | bytes 458752
  112.7 2.8 %collective-permute-start = (bf16[384,1440]{0,1:T(8,128)(2,1)S(1)}, bf16[384,1440]{0,1:T(8,128)(2,1)S(1)}, u32[]{:S(2)}, u32[]{:S(2)}) collective-permute-start(bf16[384,1440]{0,1:T(8,128)(2,1)S(1)} %constant_dynamic-slice_fusion), channel_id=1, source_target_pairs={{0,1},{1,0},{2,3},{3,2},{4,5},{5,4},{6,7},{7,6},{8,9},{9,8},{10,11... | collective-permute-start | bytes 3317768 | tf_op jit(solution)/shard_map/ppermute | solution.py:209
  115.8 5.6 %copy-start.4 = (f32[2,24,4]{1,2,0:T(4,128)S(1)}, f32[2,24,4]{1,2,0:T(4,128)}, u32[]{:S(2)}) copy-start(f32[2,24,4]{1,2,0:T(4,128)} %param.21) | copy-start | bytes 2308
  115.8 5.6 %copy-start.5 = (s32[2,24,4]{1,2,0:T(4,128)S(1)}, s32[2,24,4]{1,2,0:T(4,128)}, u32[]{:S(2)}) copy-start(s32[2,24,4]{1,2,0:T(4,128)} %param.20) | copy-start | bytes 2308
  117.8 32.6 %all-to-all-start = ((bf16[8,48,1440]{2,1,0:T(8,128)(2,1)}), bf16[8,48,1440]{2,1,0:T(8,128)(2,1)S(1)}, u32[]{:S(2)}, u32[]{:S(2)}) async-start(bf16[8,48,1440]{2,1,0:T(8,128)(2,1)} %bitcast.12), calls=%async_computation | async-start | bytes 2359296 | tf_op jit(solution)/shard_map/all_to_all | solution.py:211
Sparse Core Ops, SparseCore 0:
  23.3 53.6 all-gather.1

commit v2 on v1

--- a/solution.py
+++ b/solution.py
@@ -1,6 +1,9 @@
+import functools
 import jax
 import jax.numpy as jnp
 from jax import lax
+from jax.experimental import pallas as pl
+from jax.experimental.pallas import tpu as pltpu
 from jax.sharding import PartitionSpec as P
 
 D = 2880
@@ -162,6 +165,273 @@
     return mixed.transpose(2, 0, 1, 3, 4).reshape(STEPS * row_count, -1)
 
 
+WIDE = 3072
+HALF = WIDE // 2
+LANES = 128
+SHARE_AT = WIDE - LANES
+PAIRS = 192
+
+
+def expert_kernel(
+    zs,
+    experts,
+    rows_ref,
+    hidden_ref,
+    w_in_hbm,
+    w_down_hbm,
+    out_ref,
+    w_in,
+    w_down,
+    w_gate,
+    w_up,
+    w_half,
+    slots,
+    act,
+    kept,
+    sib_out,
+    sib_in,
+    x_out,
+    x_in,
+    z_out,
+    z_in,
+    load_sem,
+    own_send,
+    own_recv,
+    pass_send,
+    core_send,
+    core_recv,
+    sib_send,
+    sib_recv,
+    xs_send,
+    xs_recv,
+    zs_send,
+    zs_recv,
+):
+    group, me, core = lax.axis_index("groups"), lax.axis_index("expert"), lax.axis_index("tensor")
+    z, x = me // 2, me % 2
+    own_width = out_ref.shape[1]
+    both = rows_ref.shape[0]
+    width = 2 * own_width
+    hidden_local = w_gate.shape[1]
+
+    def device(to_z, to_x, to_core):
+        return (group, to_z * 2 + to_x, to_core)
+
+    peers = [device(lax.rem(z + d, zs), x, core) for d in range(1, zs)]
+    other_x = device(z, 1 - x, core)
+    other_core = device(z, x, 1 - core)
+    barrier = pltpu.get_barrier_semaphore()
+    for peer in peers + [other_x, other_core]:
+        pl.semaphore_signal(barrier, inc=1, device_id=peer, device_id_type=pl.DeviceIdType.MESH)
+    load_in = pltpu.make_async_copy(w_in_hbm, w_in, load_sem.at[0])
+    load_in.start()
+    load_down = pltpu.make_async_copy(w_down_hbm, w_down, load_sem.at[1])
+    load_down.start()
+    mine = x * zs + z
+    slots[mine] = rows_ref[...]
+    pl.semaphore_wait(barrier, zs + 1)
+
+    def remote(src, dst, send, recv, to):
+        return pltpu.make_async_remote_copy(
+            src_ref=src,
+            dst_ref=dst,
+            send_sem=send,
+            recv_sem=recv,
+            device_id=to,
+            device_id_type=pl.DeviceIdType.MESH,
+        )
+
+    def part(slot, half):
+        return slots.at[slot, :, pl.ds(pl.multiple_of(half * HALF, HALF), HALF)]
+
+    started = []
+
+    def spread(slot, send, recv, to):
+        copy = remote(part(slot, core), part(slot, core), send, recv.at[slot], to)
+        copy.start()
+        started.append(copy)
+
+    def arrived(slot, half, recv):
+        remote(part(slot, half), part(slot, half), own_send.at[0], recv.at[slot], other_x).wait_recv()
+
+    spread(mine, own_send.at[0], own_recv, other_x)
+    for d in range(1, zs):
+        spread(mine, own_send.at[d], own_recv, peers[d - 1])
+
+    row = lax.broadcasted_iota(jnp.int32, (PAIRS, 2 * PAIRS), 0)
+    column = lax.broadcasted_iota(jnp.int32, (PAIRS, 2 * PAIRS), 1)
+    evens = jnp.where(column == 2 * row, 1.0, 0.0).astype(jnp.bfloat16)
+    odds = jnp.where(column == 2 * row + 1, 1.0, 0.0).astype(jnp.bfloat16)
+
+    def separate(start, stop):
+        def one(i, carry):
+            block = w_in[pl.ds(pl.multiple_of(i * 2 * PAIRS, 2 * PAIRS), 2 * PAIRS), :]
+            at = pl.ds(pl.multiple_of(i * PAIRS, PAIRS), PAIRS)
+            w_gate[at, :] = jnp.dot(evens, block, preferred_element_type=jnp.float32).astype(
+                jnp.bfloat16
+            )
+            w_up[at, :] = jnp.dot(odds, block, preferred_element_type=jnp.float32).astype(
+                jnp.bfloat16
+            )
+            return carry
+
+        lax.fori_loop(start, stop, one, 0)
+
+    blocks = width // PAIRS
+    load_in.wait()
+    for d in range(1, zs):
+        separate(blocks * (d - 1) // (zs - 1), blocks * d // (zs - 1))
+        slot = x * zs + lax.rem(z + zs - d, zs)
+        arrived(slot, core, own_recv)
+        spread(slot, pass_send.at[d], own_recv, other_x)
+        spread(slot, core_send.at[d], core_recv, other_core)
+    load_down.wait()
+
+    def widen(i, carry):
+        at = pl.ds(pl.multiple_of(i * 96, 96), 96)
+        zeros = jnp.zeros((96, HALF - own_width), jnp.bfloat16)
+        w_half[0, at, :] = jnp.concatenate([w_down[at, :own_width], zeros], axis=1)
+        w_half[1, at, :] = jnp.concatenate([w_down[at, own_width:], zeros], axis=1)
+        return carry
+
+    lax.fori_loop(0, hidden_local // 96, widen, 0)
+
+    def first(side, at_x):
+        def one(c, carry):
+            at = pl.ds(pl.multiple_of(c * 256, 256), 256)
+            inputs = slots[pl.ds(at_x * zs, zs), :, :width].reshape(zs * both, width)
+            gate = jnp.dot(inputs, w_gate[:, at], preferred_element_type=jnp.float32)
+            up = jnp.dot(inputs, w_up[:, at], preferred_element_type=jnp.float32)
+            value = gate * jax.nn.sigmoid(1.702 * gate) * (up + 1.0)
+            act[side, :, at] = value.astype(jnp.bfloat16)
+            return carry
+
+        lax.fori_loop(0, hidden_local // 256, one, 0)
+
+    for d in range(1, zs):
+        arrived(x * zs + lax.rem(z + zs - d, zs), 1 - core, core_recv)
+    first(0, x)
+    for d in range(zs):
+        slot = (1 - x) * zs + lax.rem(z + zs - d, zs)
+        arrived(slot, core, own_recv)
+        spread(slot, core_send.at[zs + d], core_recv, other_core)
+    for d in range(zs):
+        arrived((1 - x) * zs + lax.rem(z + zs - d, zs), 1 - core, core_recv)
+    first(1, 1 - x)
+
+    def second(side, at_x):
+        lane = lax.broadcasted_iota(jnp.int32, (1, LANES), 1)
+        taken = (lax.rem(lane, experts) == me) & (lane < 3 * experts)
+        shares = slots[pl.ds(at_x * zs, zs), :, SHARE_AT:].reshape(zs * both, LANES)
+        share = jnp.sum(jnp.where(taken, shares.astype(jnp.float32), 0.0), axis=1, keepdims=True)
+
+        def tile(c, carry):
+            at = pl.ds(pl.multiple_of(c * 512, 512), 512)
+            given = jnp.dot(act[side], w_half[1 - core, :, at], preferred_element_type=jnp.float32)
+            given = (given * share).astype(jnp.bfloat16)
+            sib_out[side, :, :, at] = given.reshape(zs, both, 512)
+            return carry
+
+        def own_tile(c, carry):
+            at = pl.ds(pl.multiple_of(c * 512, 512), 512)
+            own = jnp.dot(act[side], w_half[core, :, at], preferred_element_type=jnp.float32)
+            kept[side, :, :, at] = (own * share).reshape(zs, both, 512)
+            return carry
+
+        lax.fori_loop(0, HALF // 512, tile, 0)
+        copy = remote(
+            sib_out.at[side], sib_in.at[side], sib_send.at[side], sib_recv.at[side], other_core
+        )
+        copy.start()
+        lax.fori_loop(0, HALF // 512, own_tile, 0)
+        return copy
+
+    across = second(1, 1 - x)
+    across.wait_recv()
+    started.append(across)
+    x_copies = []
+    for d in range(zs):
+        to_z = lax.rem(z + d + 1, zs)
+        x_out[d] = (kept[1, to_z] + sib_in[1, to_z].astype(jnp.float32)).astype(jnp.bfloat16)
+        copy = remote(x_out.at[d], x_in.at[d], xs_send.at[d], xs_recv.at[d], other_x)
+        copy.start()
+        x_copies.append(copy)
+        started.append(copy)
+    along = second(0, x)
+    along.wait_recv()
+    started.append(along)
+    z_copies = []
+    for d in range(zs):
+        to_z = lax.rem(z + d + 1, zs)
+        x_copies[d].wait_recv()
+        total = kept[0, to_z] + sib_in[0, to_z].astype(jnp.float32) + x_in[d].astype(jnp.float32)
+        if d < zs - 1:
+            z_out[d] = total.astype(jnp.bfloat16)
+            copy = remote(z_out.at[d], z_in.at[d], zs_send.at[d], zs_recv.at[d], peers[d])
+            copy.start()
+            z_copies.append(copy)
+            started.append(copy)
+    for d in range(zs - 1):
+        z_copies[d].wait_recv()
+        total = total + z_in[d].astype(jnp.float32)
+    out_ref[...] = (hidden_ref[...].astype(jnp.float32) + total[:, :own_width]).astype(
+        out_ref.dtype
+    )
+    for copy in started:
+        copy.wait_send()
+
+
+def run_experts(rows, hidden_own, w_in, w_down, experts):
+    both, own_width = hidden_own.shape
+    zs = experts // 2
+    hidden_local, width = w_down.shape
+    bf16, dma = jnp.bfloat16, pltpu.SemaphoreType.DMA
+    vmem = pl.BlockSpec(memory_space=pltpu.VMEM)
+    anywhere = pl.BlockSpec(memory_space=pl.ANY)
+    return pl.pallas_call(
+        functools.partial(expert_kernel, zs, experts),
+        out_shape=jax.ShapeDtypeStruct((both, own_width), bf16),
+        in_specs=[vmem, vmem, anywhere, anywhere],
+        out_specs=vmem,
+        scratch_shapes=[
+            pltpu.VMEM(w_in.shape, bf16),
+            pltpu.VMEM(w_down.shape, bf16),
+            pltpu.VMEM((width, hidden_local), bf16),
+            pltpu.VMEM((width, hidden_local), bf16),
+            pltpu.VMEM((2, hidden_local, HALF), bf16),
+            pltpu.VMEM((experts, both, WIDE), bf16),
+            pltpu.VMEM((2, zs * both, hidden_local), bf16),
+            pltpu.VMEM((2, zs, both, HALF), jnp.float32),
+            pltpu.VMEM((2, zs, both, HALF), bf16),
+            pltpu.VMEM((2, zs, both, HALF), bf16),
+            pltpu.VMEM((zs, both, HALF), bf16),
+            pltpu.VMEM((zs, both, HALF), bf16),
+            pltpu.VMEM((zs - 1, both, HALF), bf16),
+            pltpu.VMEM((zs - 1, both, HALF), bf16),
+            dma((2,)),
+            dma((zs,)),
+            dma((experts,)),
+            dma((zs,)),
+            dma((experts,)),
+            dma((experts,)),
+            dma((2,)),
+            dma((2,)),
+            dma((zs,)),
+            dma((zs,)),
+            dma((zs - 1,)),
+            dma((zs - 1,)),
+        ],
+        compiler_params=pltpu.CompilerParams(
+            collective_id=0, has_side_effects=True, vmem_limit_bytes=56 * 2**20
+        ),
+        cost_estimate=pl.CostEstimate(
+            flops=6 * experts * both * width * hidden_local,
+            bytes_accessed=14 * 2**20,
+            transcendentals=0,
+        ),
+    )(rows, hidden_own, w_in, w_down)
+
+
 def body_dense(
     residual,
     queries,
@@ -192,29 +462,18 @@
     inv_rms = lax.rsqrt(jnp.mean(widened * widened, axis=1, keepdims=True) + 1e-05)
     normed = (widened * inv_rms * norm_gain.astype(jnp.float32)).astype(jnp.bfloat16)
     hidden_own = lax.dynamic_slice_in_dim(hidden_full, col_start, own_width, 1)
-    gathered = lax.all_gather(normed, "expert", axis=0, tiled=True)
-    w_in = w_gate_up.reshape(2 * D, hidden_local)
-    twice = jnp.repeat(gathered, 2, axis=1)
-    even = jnp.arange(2 * D, dtype=jnp.int32)[None, :] % 2 == 0
-    placed = jnp.concatenate([jnp.where(even, twice, 0), jnp.where(even, 0, twice)], axis=0)
-    gate_up = jnp.dot(placed, w_in, preferred_element_type=jnp.float32)
-    gate_part, up_part = gate_up[: experts * both], gate_up[experts * both :]
-    activation = (gate_part * jax.nn.sigmoid(1.702 * gate_part) * (up_part + 1.0)).astype(
-        jnp.bfloat16
-    )
-    partial_out = jnp.dot(activation, w_down[0], preferred_element_type=jnp.float32)
-    partial_out = partial_out.astype(jnp.bfloat16)
-    kept = lax.dynamic_slice_in_dim(partial_out, col_start, own_width, 1)
-    given = lax.dynamic_slice_in_dim(partial_out, own_width - col_start, own_width, 1)
-    got = lax.ppermute(given, "tensor", [(0, 1), (1, 0)])
-    summed = (kept.astype(jnp.float32) + got.astype(jnp.float32)).astype(jnp.bfloat16)
-    returned = lax.all_to_all(
-        summed.reshape(experts, both, own_width), "expert", split_axis=0, concat_axis=0, tiled=True
-    )
     named = expert_ids[..., None] == jnp.arange(experts, dtype=jnp.int32)
     share = jnp.sum(jnp.where(named, gate_weights[..., None], 0.0), axis=2).reshape(both, experts)
-    mixture = jnp.sum(returned.astype(jnp.float32) * share.T[:, :, None], axis=0)
-    out = (hidden_own.astype(jnp.float32) + mixture).astype(jnp.bfloat16)
+    pieces = []
+    for unused in range(3):
+        piece = lax.reduce_precision(share, 8, 7)
+        pieces.append(piece.astype(jnp.bfloat16))
+        share = share - piece
+    rows = jnp.concatenate([normed, jnp.zeros((both, SHARE_AT - D), jnp.bfloat16)] + pieces, axis=1)
+    rows = jnp.pad(rows, ((0, 0), (0, WIDE - rows.shape[1])))
+    out = run_experts(
+        rows, hidden_own, w_gate_up.reshape(2 * D, hidden_local), w_down[0], experts
+    )
     return out.reshape(STEPS, row_count, own_width)
 
 

time: 159 us -> 101 us (0.64)
  waiting for transfers between devices: 66.6 us -> 0 us
  Pallas kernels: 0 us -> 51.2 us
  between operations: 13.7 us -> 0.16 us
  matrix products: 19.2 us -> 5.74 us
  local copies, waits for them, and re-layouts: 41.9 us -> 35.1 us
  other arithmetic: 8.4 us -> 3.18 us
  starting transfers between devices: 3.67 us -> 0 us
    pallas_call x0 -> x1, Pallas kernels: none -> 51.2 us  [run_experts(): pl.pallas_call(functools.partial(expert_kernel, zs, experts), out_shape=j...]
    all_gather x1 -> x0, waiting for transfers between devices: 34.9 us -> none  [body_dense(): gathered = lax.all_gather(normed, 'expert', axis=0, tiled=True)]
    all_to_all x1 -> x0, waiting for transfers between devices: 28.9 us -> none  [body_dense(): lax.all_to_all(summed.reshape(experts, both, own_width), 'expert', split_...]
    dot_general x2 -> x0, matrix products: 13.5 us -> none  [the longest x1 10.9 us: body_dense(): gate_up = jnp.dot(placed, w_in, preferred_element_type=jnp.float32)]
    reshape x3 -> x1, local copies, waits for them, and re-layouts: 29.1 us -> 18.9 us  [body_dense(): w_gate_up.reshape(2 * D, hidden_local)]
    unnamed x22 -> x6, local copies, waits for them, and re-layouts: 0.07 us -> 8.18 us
    select_n x1 -> x0, other arithmetic: 5.16 us -> none  [body_dense(): jnp.where(even, twice, 0)]
    broadcast_in_dim x1, local copies, waits for them, and re-layouts: 3.74 us -> 0.01 us  [body_dense(): jnp.zeros((both, SHARE_AT - D), jnp.bfloat16)]
  transfers between devices with their start and end apart: 3 -> 0, of which waited for: 3 -> 0; matrix products, arithmetic and copies ran while one was open for 12% -> 0% of each run, Pallas kernels for 0% -> 0%
where the time goes in v2:
time: 101 us; the launch traced here: 100 us
  Pallas kernels  51.2 us (51%)
  local copies, waits for them, and re-layouts  35.1 us (35%)
  matrix products  5.74 us (6%)
  blocking collectives  4.85 us (5%)
  other arithmetic  3.18 us (3%)
    pallas_call x1, Pallas kernels, run_experts(): pl.pallas_call(functools.partial(expert_kernel, zs, experts), out_shape=j...  51.2 us
    reshape x1, local copies, waits for them, and re-layouts, body_dense(): w_gate_up.reshape(2 * D, hidden_local)  18.9 us
    unnamed x6, local copies, waits for them, and re-layouts  8.18 us
    psum x1, blocking collectives, body_dense(): hidden_full = lax.psum(with_input, 'tensor').astype(jnp.bfloat16)  4.85 us
    dot_general x1, matrix products, body_dense(): projected = jnp.dot(heads, out_proj, preferred_element_type=jnp.float32)  4.54 us

profile of v2, /device:TPU:0, one launch (start us, length us, event | category | flops | bytes accessed | tf_op | source)
XLA Modules:
  0.0 100.2 jit_solution(745174269192467158)
XLA Ops:
  0.0 0.1 iota_compare_fusion.2
  0.1 0.7 tile.9
  0.8 0.1 tile.11
  0.9 0.7 iota_compare_fusion.1
  1.6 0.7 select_reduce_fusion
  2.4 0.7 convert_element_type.41
  3.1 0.1 copy.42
  3.2 0.1 pad_add_fusion
  3.3 0.9 reshape.119
  4.2 0.1 copy.51
  4.3 0.1 slice_bitcast_fusion.3
  4.4 1.1 %reshape.111 = bf16[2,24,4,4,64]{4,3,2,1,0:T(4,128)(2,1)S(1)} reshape(bf16[2,24,1024]{2,1,0:T(8,128)(2,1)} %param.13) | data formatting | bytes 196608 | tf_op jit(solution)/shard_map/reshape | solution.py:145
  5.5 0.1 copy.39
  5.6 1.7 %slice_bitcast_fusion.1 = (bf16[24,4,32,64]{3,2,1,0:T(8,128)(2,1)S(1)}, bf16[24,4,32,64]{3,2,1,0:T(8,128)(2,1)S(1)}) fusion(bf16[24,2,4,32,64]{4,3,2,1,0:T(8,128)(2,1)} %param.15), kind=kLoop, calls=%fused_computation.11 | loop fusion | bytes 1572864 | tf_op jit(solution)/shard_map/squeeze | solution.py:143
  7.3 0.7 fusion.18
  8.0 0.4 fusion.11
  8.4 0.5 convolution_convert_fusion
  8.9 0.0 copy-start
  8.9 0.1 copy.50
  8.9 0.2 reshape.114
  9.1 4.5 %fusion.19 = f32[48,2880]{1,0:T(8,128)S(1)} fusion(bf16[48,1024]{1,0:T(8,128)(2,1)S(1)} %reshape.114, bf16[1024,2880]{0,1:T(8,128)(2,1)} %param.18), kind=kOutput, calls=%fused_computation.49 | convolution fusion | flops 283115520 | bytes 6549504 | tf_op jit(solution)/shard_map/dot_general | solution.py:456
  13.7 0.0 copy-done
  13.7 0.2 convert_add_fusion
  13.9 1.3 %dynamic_update_slice.3 = f32[48,2880]{1,0:T(8,128)S(1)} dynamic-update-slice(f32[48,2880]{1,0:T(8,128)S(1)} %fusion.19, f32[48,1440]{1,0:T(8,128)S(1)} %convert_add_fusion, s32[]{:T(128)} %constant.29.clone.1, s32[]{:T(128)S(6)} %select_n.24) | dynamic-update-slice | bytes 552964 | tf_op jit(solution)/shard_map/dynamic_update_slice | solution.py:459
  15.1 4.9 %all-reduce.2 = bf16[48,2880]{1,0:T(8,128)(2,1)S(1)} all-reduce(f32[48,2880]{1,0:T(8,128)S(1)} %dynamic_update_slice.3), channel_id=1, replica_groups=mesh['groups'=2,'expert'=8,'tensor'=2] {'tensor'}, use_global_device_ids=true, to_apply=%region_2.3 | all-reduce | flops 138240 | bytes 829440 | tf_op jit(solution)/shard_map/psum | solution.py:460
  20.0 0.2 fusion.8
  20.2 0.8 constant_dynamic-slice_fusion.hidden_ref
  21.0 0.1 fusion.10
  21.1 0.1 concatenate.15
  21.2 0.7 pad.4.rows_ref
  21.9 6.6 %copy.43 = bf16[1,768,2880]{2,1,0:T(8,128)(2,1)} copy(bf16[1,768,2880]{1,2,0:T(8,128)(2,1)} %param.23) | data formatting | bytes 8847360 | tf_op args[11]
  28.5 18.9 %reshape.116.w_in_hbm = bf16[5760,768]{1,0:T(8,128)(2,1)} reshape(bf16[1,2880,2,768]{3,2,1,0:T(2,128)(2,1)} %param.22) | data formatting | bytes 17694720 | tf_op jit(solution)/shard_map/reshape | solution.py:475
  47.4 51.2 %shard_map.118 = bf16[48,1440]{1,0:T(8,128)(2,1)} custom-call(bf16[48,3072]{1,0:T(8,128)(2,1)} %pad.4.rows_ref, bf16[48,1440]{1,0:T(8,128)(2,1)} %constant_dynamic-slice_fusion.hidden_ref, bf16[5760,768]{1,0:T(8,128)(2,1)} %reshape.116.w_in_hbm, bf16[768,2880]{1,0:T(8,128)(2,1)} %bitcast.47), custom_call_target="tpu_custom_call" | custom-call | flops 5096079360 | bytes 14680064 | tf_op jit(solution)/shard_map/pallas_call | solution.py:391
  98.6 1.6 %copy.56 = bf16[2,24,1440]{2,1,0:T(8,128)(2,1)} copy(bf16[2,24,1440]{2,1,0:T(8,128)(2,1)} %bitcast.58) | data formatting | bytes 276480
  (11 shorter events, 0.1 us)
Async XLA Ops:
  8.9 4.8 %copy-start = (bf16[2,24,1440]{2,1,0:T(8,128)(2,1)S(1)}, bf16[2,24,1440]{2,1,0:T(8,128)(2,1)}, u32[]{:S(2)}) copy-start(bf16[2,24,1440]{2,1,0:T(8,128)(2,1)} %param.12) | copy-start | bytes 414724

commit v3 on v2

--- a/solution.py
+++ b/solution.py
@@ -175,8 +175,10 @@
 def expert_kernel(
     zs,
     experts,
-    rows_ref,
-    hidden_ref,
+    projected_ref,
+    residual_ref,
+    gain_ref,
+    pieces_ref,
     w_in_hbm,
     w_down_hbm,
     out_ref,
@@ -184,7 +186,6 @@
     w_down,
     w_gate,
     w_up,
-    w_half,
     slots,
     act,
     kept,
@@ -206,11 +207,15 @@
     xs_recv,
     zs_send,
     zs_recv,
+    sum_out,
+    sum_in,
+    hidden_own,
+    sum_sem,
 ):
     group, me, core = lax.axis_index("groups"), lax.axis_index("expert"), lax.axis_index("tensor")
     z, x = me // 2, me % 2
     own_width = out_ref.shape[1]
-    both = rows_ref.shape[0]
+    both = projected_ref.shape[0]
     width = 2 * own_width
     hidden_local = w_gate.shape[1]
 
@@ -225,10 +230,25 @@
         pl.semaphore_signal(barrier, inc=1, device_id=peer, device_id_type=pl.DeviceIdType.MESH)
     load_in = pltpu.make_async_copy(w_in_hbm, w_in, load_sem.at[0])
     load_in.start()
-    load_down = pltpu.make_async_copy(w_down_hbm, w_down, load_sem.at[1])
+    load_down = pltpu.make_async_copy(w_down_hbm, w_down.at[pl.ds(0, width)], load_sem.at[1])
     load_down.start()
+    w_down[width:, :] = jnp.zeros((w_down.shape[0] - width, hidden_local), jnp.bfloat16)
     mine = x * zs + z
-    slots[mine] = rows_ref[...]
+
+    @pl.when(core == 0)
+    def _():
+        sum_out[:, :own_width] = projected_ref[:, :own_width] + residual_ref[...].astype(
+            jnp.float32
+        )
+        sum_out[:, own_width:] = projected_ref[:, own_width:]
+
+    @pl.when(core == 1)
+    def _():
+        sum_out[:, :own_width] = projected_ref[:, :own_width]
+        sum_out[:, own_width:] = projected_ref[:, own_width:] + residual_ref[...].astype(
+            jnp.float32
+        )
+
     pl.semaphore_wait(barrier, zs + 1)
 
     def remote(src, dst, send, recv, to):
@@ -245,6 +265,26 @@
         return slots.at[slot, :, pl.ds(pl.multiple_of(half * HALF, HALF), HALF)]
 
     started = []
+    exchange = remote(sum_out, sum_in, sum_sem.at[0], sum_sem.at[1], other_core)
+    exchange.start()
+    started.append(exchange)
+    slots[mine, :, SHARE_AT - LANES :] = jnp.zeros((both, 2 * LANES), jnp.bfloat16)
+    slots[mine, :, SHARE_AT:] = pieces_ref[...]
+    exchange.wait_recv()
+    hidden = (sum_out[...] + sum_in[...]).astype(jnp.bfloat16)
+
+    @pl.when(core == 0)
+    def _():
+        hidden_own[...] = hidden[:, :own_width]
+
+    @pl.when(core == 1)
+    def _():
+        hidden_own[...] = hidden[:, own_width:]
+
+    widened = hidden.astype(jnp.float32)
+    inv_rms = lax.rsqrt(jnp.mean(widened * widened, axis=1, keepdims=True) + 1e-05)
+    normed = widened * inv_rms * gain_ref[...].astype(jnp.float32)
+    slots[mine, :, :width] = normed.astype(jnp.bfloat16)
 
     def spread(slot, send, recv, to):
         copy = remote(part(slot, core), part(slot, core), send, recv.at[slot], to)
@@ -265,8 +305,8 @@
 
     def separate(start, stop):
         def one(i, carry):
-            block = w_in[pl.ds(pl.multiple_of(i * 2 * PAIRS, 2 * PAIRS), 2 * PAIRS), :]
             at = pl.ds(pl.multiple_of(i * PAIRS, PAIRS), PAIRS)
+            block = w_in[at, :, :].reshape(2 * PAIRS, hidden_local)
             w_gate[at, :] = jnp.dot(evens, block, preferred_element_type=jnp.float32).astype(
                 jnp.bfloat16
             )
@@ -286,15 +326,6 @@
         spread(slot, pass_send.at[d], own_recv, other_x)
         spread(slot, core_send.at[d], core_recv, other_core)
     load_down.wait()
-
-    def widen(i, carry):
-        at = pl.ds(pl.multiple_of(i * 96, 96), 96)
-        zeros = jnp.zeros((96, HALF - own_width), jnp.bfloat16)
-        w_half[0, at, :] = jnp.concatenate([w_down[at, :own_width], zeros], axis=1)
-        w_half[1, at, :] = jnp.concatenate([w_down[at, own_width:], zeros], axis=1)
-        return carry
-
-    lax.fori_loop(0, hidden_local // 96, widen, 0)
 
     def first(side, at_x):
         def one(c, carry):
@@ -325,17 +356,24 @@
         shares = slots[pl.ds(at_x * zs, zs), :, SHARE_AT:].reshape(zs * both, LANES)
         share = jnp.sum(jnp.where(taken, shares.astype(jnp.float32), 0.0), axis=1, keepdims=True)
 
+        def outputs(half, c):
+            start = pl.multiple_of(half * own_width + c * 512, 16)
+            return lax.dot_general(
+                act[side],
+                w_down[pl.ds(start, 512), :],
+                (((1,), (1,)), ((), ())),
+                preferred_element_type=jnp.float32,
+            )
+
         def tile(c, carry):
             at = pl.ds(pl.multiple_of(c * 512, 512), 512)
-            given = jnp.dot(act[side], w_half[1 - core, :, at], preferred_element_type=jnp.float32)
-            given = (given * share).astype(jnp.bfloat16)
+            given = (outputs(1 - core, c) * share).astype(jnp.bfloat16)
             sib_out[side, :, :, at] = given.reshape(zs, both, 512)
             return carry
 
         def own_tile(c, carry):
             at = pl.ds(pl.multiple_of(c * 512, 512), 512)
-            own = jnp.dot(act[side], w_half[core, :, at], preferred_element_type=jnp.float32)
-            kept[side, :, :, at] = (own * share).reshape(zs, both, 512)
+            kept[side, :, :, at] = (outputs(core, c) * share).reshape(zs, both, 512)
             return carry
 
         lax.fori_loop(0, HALF // 512, tile, 0)
@@ -374,31 +412,30 @@
     for d in range(zs - 1):
         z_copies[d].wait_recv()
         total = total + z_in[d].astype(jnp.float32)
-    out_ref[...] = (hidden_ref[...].astype(jnp.float32) + total[:, :own_width]).astype(
+    out_ref[...] = (hidden_own[...].astype(jnp.float32) + total[:, :own_width]).astype(
         out_ref.dtype
     )
     for copy in started:
         copy.wait_send()
 
 
-def run_experts(rows, hidden_own, w_in, w_down, experts):
-    both, own_width = hidden_own.shape
+def run_experts(projected, residual, gain, pieces, w_in, w_down, experts):
+    both, own_width = residual.shape
     zs = experts // 2
-    hidden_local, width = w_down.shape
+    width, hidden_local = w_down.shape
     bf16, dma = jnp.bfloat16, pltpu.SemaphoreType.DMA
     vmem = pl.BlockSpec(memory_space=pltpu.VMEM)
     anywhere = pl.BlockSpec(memory_space=pl.ANY)
     return pl.pallas_call(
         functools.partial(expert_kernel, zs, experts),
         out_shape=jax.ShapeDtypeStruct((both, own_width), bf16),
-        in_specs=[vmem, vmem, anywhere, anywhere],
+        in_specs=[vmem, vmem, vmem, vmem, anywhere, anywhere],
         out_specs=vmem,
         scratch_shapes=[
             pltpu.VMEM(w_in.shape, bf16),
-            pltpu.VMEM(w_down.shape, bf16),
+            pltpu.VMEM((own_width + HALF, hidden_local), bf16),
             pltpu.VMEM((width, hidden_local), bf16),
             pltpu.VMEM((width, hidden_local), bf16),
-            pltpu.VMEM((2, hidden_local, HALF), bf16),
             pltpu.VMEM((experts, both, WIDE), bf16),
             pltpu.VMEM((2, zs * both, hidden_local), bf16),
             pltpu.VMEM((2, zs, both, HALF), jnp.float32),
@@ -420,6 +457,10 @@
             dma((zs,)),
             dma((zs - 1,)),
             dma((zs - 1,)),
+            pltpu.VMEM((both, width), jnp.float32),
+            pltpu.VMEM((both, width), jnp.float32),
+            pltpu.VMEM((both, own_width), bf16),
+            dma((2,)),
         ],
         compiler_params=pltpu.CompilerParams(
             collective_id=0, has_side_effects=True, vmem_limit_bytes=56 * 2**20
@@ -429,7 +470,7 @@
             bytes_accessed=14 * 2**20,
             transcendentals=0,
         ),
-    )(rows, hidden_own, w_in, w_down)
+    )(projected, residual, gain, pieces, w_in, w_down)
 
 
 def body_dense(
@@ -449,19 +490,9 @@
     row_count, own_width = residual.shape[1:]
     experts = lax.axis_size("expert")
     both = STEPS * row_count
-    hidden_local = w_down.shape[1]
-    col_start = lax.axis_index("tensor") * own_width
     valid = jnp.arange(CACHE, dtype=jnp.int32)[None, :] < lengths[:, None]
     heads = attend_steps(queries, new_kv, kv_cache, valid, sink_logits)
     projected = jnp.dot(heads, out_proj, preferred_element_type=jnp.float32)
-    own_cols = lax.dynamic_slice_in_dim(projected, col_start, own_width, 1)
-    own_cols = own_cols + residual.reshape(both, own_width).astype(jnp.float32)
-    with_input = lax.dynamic_update_slice_in_dim(projected, own_cols, col_start, 1)
-    hidden_full = lax.psum(with_input, "tensor").astype(jnp.bfloat16)
-    widened = lax.optimization_barrier(hidden_full).astype(jnp.float32)
-    inv_rms = lax.rsqrt(jnp.mean(widened * widened, axis=1, keepdims=True) + 1e-05)
-    normed = (widened * inv_rms * norm_gain.astype(jnp.float32)).astype(jnp.bfloat16)
-    hidden_own = lax.dynamic_slice_in_dim(hidden_full, col_start, own_width, 1)
     named = expert_ids[..., None] == jnp.arange(experts, dtype=jnp.int32)
     share = jnp.sum(jnp.where(named, gate_weights[..., None], 0.0), axis=2).reshape(both, experts)
     pieces = []
@@ -469,10 +500,16 @@
         piece = lax.reduce_precision(share, 8, 7)
         pieces.append(piece.astype(jnp.bfloat16))
         share = share - piece
-    rows = jnp.concatenate([normed, jnp.zeros((both, SHARE_AT - D), jnp.bfloat16)] + pieces, axis=1)
-    rows = jnp.pad(rows, ((0, 0), (0, WIDE - rows.shape[1])))
+    pieces = jnp.concatenate(pieces, axis=1)
+    pieces = jnp.pad(pieces, ((0, 0), (0, LANES - pieces.shape[1])))
     out = run_experts(
-        rows, hidden_own, w_gate_up.reshape(2 * D, hidden_local), w_down[0], experts
+        projected,
+        residual.reshape(both, own_width),
+        norm_gain[None],
+        pieces,
+        w_gate_up[0],
+        w_down[0].T,
+        experts,
     )
     return out.reshape(STEPS, row_count, own_width)
 

time: 101 us -> 68.1 us (0.67)
  local copies, waits for them, and re-layouts: 35.1 us -> 5.79 us
  blocking collectives: 4.85 us -> 0 us
  Pallas kernels: 51.2 us -> 54 us
  other arithmetic: 3.18 us -> 1.35 us
    reshape x1 -> x0, local copies, waits for them, and re-layouts: 18.9 us -> none  [body_dense(): w_gate_up.reshape(2 * D, hidden_local)]
    unnamed x6 -> x15, local copies, waits for them, and re-layouts: 8.18 us -> 1.62 us
    psum x1 -> x0, blocking collectives: 4.85 us -> none  [body_dense(): hidden_full = lax.psum(with_input, 'tensor').astype(jnp.bfloat16)]
    pallas_call x1, Pallas kernels: 51.2 us -> 54 us  [run_experts(): pl.pallas_call(functools.partial(expert_kernel, zs, experts), out_shape=j...]
    dynamic_update_slice x1 -> x0, local copies, waits for them, and re-layouts: 1.28 us -> none  [body_dense(): lax.dynamic_update_slice_in_dim(projected, own_cols, col_start, 1)]
where the time goes in v3:
time: 68.1 us; the launch traced here: 67.9 us
  Pallas kernels  54 us (79%)
  matrix products  6.55 us (10%)
  local copies, waits for them, and re-layouts  5.79 us (9%)
  other arithmetic  1.35 us (2%)
    pallas_call x1, Pallas kernels, run_experts(): pl.pallas_call(functools.partial(expert_kernel, zs, experts), out_shape=j...  54 us
    dot_general x1, matrix products, body_dense(): projected = jnp.dot(heads, out_proj, preferred_element_type=jnp.float32)  5.38 us
    squeeze x2, local copies, waits for them, and re-layouts, attend_steps(): key_all = jnp.concatenate([kv_cache[:, 0], fresh[0]], axis=2)  1.73 us
    unnamed x15, local copies, waits for them, and re-layouts  1.62 us

profile of v3, /device:TPU:0, one launch (start us, length us, event | category | flops | bytes accessed | tf_op | source)
XLA Modules:
  0.0 67.9 jit_solution(1267314930624763019)
XLA Ops:
  0.0 0.0 copy-start
  0.0 1.0 %reshape.106 = bf16[2,24,2,4,64]{4,3,2,1,0:T(4,128)(2,1)S(1)} reshape(bf16[2,24,2,256]{3,2,1,0:T(2,128)(2,1)} %param.14) | data formatting | bytes 98304 | tf_op jit(solution)/shard_map/reshape | solution.py:142
  1.0 0.1 copy.47
  1.1 0.1 slice_bitcast_fusion.3
  1.2 0.0 copy-start.4
  1.2 1.7 %slice_bitcast_fusion.1 = (bf16[24,4,32,64]{3,2,1,0:T(8,128)(2,1)S(1)}, bf16[24,4,32,64]{3,2,1,0:T(8,128)(2,1)S(1)}) fusion(bf16[24,2,4,32,64]{4,3,2,1,0:T(8,128)(2,1)} %param.15), kind=kLoop, calls=%fused_computation.11 | loop fusion | bytes 1572864 | tf_op jit(solution)/shard_map/squeeze | solution.py:143
  2.8 0.0 copy-start.5
  2.8 0.0 copy-done
  2.9 0.2 reshape.99
  3.0 0.1 copy.36
  3.1 0.1 iota_compare_fusion.3
  3.2 0.0 copy-done.4
  3.2 0.1 iota_compare_fusion.2
  3.3 0.1 pad_add_fusion
  3.4 0.7 %fusion.20 = (f32[24,4,8]{2,1,0:T(4,128)S(1)}, f32[24,4,8,34]{3,2,1,0:T(8,128)S(1)}) fusion(bf16[24,4,8,64]{3,2,1,0:T(8,128)(2,1)S(1)} %bitcast.51, bf16[24,4,2,64]{3,2,1,0:T(2,128)(2,1)S(1)} %get-tuple-element.7, bf16[24,4,32,64]{3,2,1,0:T(8,128)(2,1)S(1)} %get-tuple-element.5, pred[24,8,34]{2,1,0:T(8,128)(4,1)S(1)} %pad_add_fusion), kind=kOutput, calls=%fused_computation.46 | convolution fusion | flops 4255488 | bytes 630144 | tf_op jit(solution)/shard_map/rkgd,rkjd->rkgj/dot_general | solution.py:156
  4.1 0.0 copy-done.5
  4.1 0.1 tile.9
  4.2 0.1 tile.11
  4.3 0.4 fusion.8
  4.7 0.4 convolution_convert_fusion
  5.2 0.1 copy.46
  5.3 0.2 reshape.102
  5.4 0.0 copy-start.1
  5.5 0.0 copy-start.2
  5.5 0.0 copy-start.3
  5.5 5.4 %fusion.21.projected_ref = f32[48,2880]{1,0:T(8,128)} fusion(bf16[48,1024]{1,0:T(8,128)(2,1)S(1)} %reshape.102, bf16[1024,2880]{0,1:T(8,128)(2,1)} %param.18), kind=kOutput, calls=%fused_computation.47 | convolution fusion | flops 283115520 | bytes 6549504 | tf_op jit(solution)/shard_map/dot_general | solution.py:495
  10.9 0.0 copy-done.1
  10.9 0.6 broadcast_in_dim.34.gain_ref
  11.5 0.0 copy-done.2
  11.5 0.0 copy-done.3
  11.5 0.1 copy.39
  11.6 0.7 %fusion.17.pieces_ref = bf16[48,128]{1,0:T(8,128)(2,1)} fusion(bf16[48,8]{1,0:T(8,128)(2,1)S(1)} %get-tuple-element.10, bf16[48,8]{1,0:T(8,128)(2,1)S(1)} %get-tuple-element.11, bf16[48,8]{1,0:T(8,128)(2,1)S(1)} %get-tuple-element.9), kind=kLoop, calls=%fused_computation.37 | loop fusion | flops 61440 | bytes 14592 | tf_op jit(solution)/shard_map/concatenate | solution.py:503
  12.3 54.0 %shard_map.118 = bf16[48,1440]{1,0:T(8,128)(2,1)} custom-call(f32[48,2880]{1,0:T(8,128)} %fusion.21.projected_ref, bf16[48,1440]{1,0:T(8,128)(2,1)} %bitcast.64, bf16[1,2880]{1,0:T(2,128)(2,1)} %broadcast_in_dim.34.gain_ref, bf16[48,128]{1,0:T(8,128)(2,1)} %fusion.17.pieces_ref, bf16[2880,2,768]{2,1,0:T(2,128)(2,1)} %bitcast.62, bf16[2880,768]{1,0:T(8,128)(2,1)} %bitcast.63), custom_call_target="tpu_custom_call" | custom-call | flops 5096079360 | bytes 14680064 | tf_op jit(solution)/shard_map/pallas_call | solution.py:429
  66.3 1.6 %copy.49 = bf16[2,24,1440]{2,1,0:T(8,128)(2,1)} copy(bf16[2,24,1440]{2,1,0:T(8,128)(2,1)} %bitcast.58) | data formatting | bytes 276480
  (10 shorter events, 0.1 us)
Async XLA Ops:
  0.0 2.9 %copy-start = (bf16[2,24,1024]{2,1,0:T(8,128)(2,1)S(1)}, bf16[2,24,1024]{2,1,0:T(8,128)(2,1)}, u32[]{:S(2)}) copy-start(bf16[2,24,1024]{2,1,0:T(8,128)(2,1)} %param.13) | copy-start | bytes 294916
  1.2 2.0 %copy-start.4 = (s32[24]{0:T(128)S(1)}, s32[24]{0:T(128)}, u32[]{:S(2)}) copy-start(s32[24]{0:T(128)} %param.16) | copy-start | bytes 292
  2.8 1.3 %copy-start.5 = (f32[16]{0:T(128)S(1)}, f32[16]{0:T(128)}, u32[]{:S(2)}) copy-start(f32[16]{0:T(128)} %param.17) | copy-start | bytes 196
  5.4 5.4 %copy-start.1 = (bf16[2880]{0:T(1024)(128)(2,1)S(1)}, bf16[2880]{0:T(1024)(128)(2,1)}, u32[]{:S(2)}) copy-start(bf16[2880]{0:T(1024)(128)(2,1)} %param.19) | copy-start | bytes 17284
  5.5 6.0 %copy-start.2 = (f32[2,24,4]{1,2,0:T(4,128)S(1)}, f32[2,24,4]{1,2,0:T(4,128)}, u32[]{:S(2)}) copy-start(f32[2,24,4]{1,2,0:T(4,128)} %param.21) | copy-start | bytes 2308
  5.5 6.0 %copy-start.3 = (s32[2,24,4]{1,2,0:T(4,128)S(1)}, s32[2,24,4]{1,2,0:T(4,128)}, u32[]{:S(2)}) copy-start(s32[2,24,4]{1,2,0:T(4,128)} %param.20) | copy-start | bytes 2308

commit v4 on v3

--- a/solution.py
+++ b/solution.py
@@ -341,11 +341,16 @@
 
     for d in range(1, zs):
         arrived(x * zs + lax.rem(z + zs - d, zs), 1 - core, core_recv)
+
+    def relay(start, stop):
+        for d in range(start, stop):
+            slot = (1 - x) * zs + lax.rem(z + zs - d, zs)
+            arrived(slot, core, own_recv)
+            spread(slot, core_send.at[zs + d], core_recv, other_core)
+
+    relay(0, zs // 2)
     first(0, x)
-    for d in range(zs):
-        slot = (1 - x) * zs + lax.rem(z + zs - d, zs)
-        arrived(slot, core, own_recv)
-        spread(slot, core_send.at[zs + d], core_recv, other_core)
+    relay(zs // 2, zs)
     for d in range(zs):
         arrived((1 - x) * zs + lax.rem(z + zs - d, zs), 1 - core, core_recv)
     first(1, 1 - x)

time: 68.1 us -> 68.1 us (level)
  no operation moved by 1% of the time
where the time goes in v4:
time: 68.1 us; the launch traced here: 67.9 us
  Pallas kernels  54 us (79%)
  matrix products  6.55 us (10%)
  local copies, waits for them, and re-layouts  5.79 us (9%)
  other arithmetic  1.35 us (2%)
    pallas_call x1, Pallas kernels, run_experts(): pl.pallas_call(functools.partial(expert_kernel, zs, experts), out_shape=j...  54 us
    dot_general x1, matrix products, body_dense(): projected = jnp.dot(heads, out_proj, preferred_element_type=jnp.float32)  5.38 us
    squeeze x2, local copies, waits for them, and re-layouts, attend_steps(): key_all = jnp.concatenate([kv_cache[:, 0], fresh[0]], axis=2)  1.73 us
    unnamed x15, local copies, waits for them, and re-layouts  1.62 us

profile of v4, /device:TPU:0, one launch (start us, length us, event | category | flops | bytes accessed | tf_op | source)
XLA Modules:
  0.0 67.9 jit_solution(10056384530387388982)
XLA Ops:
  0.0 0.0 copy-start
  0.0 1.0 %reshape.106 = bf16[2,24,2,4,64]{4,3,2,1,0:T(4,128)(2,1)S(1)} reshape(bf16[2,24,2,256]{3,2,1,0:T(2,128)(2,1)} %param.14) | data formatting | bytes 98304 | tf_op jit(solution)/shard_map/reshape | solution.py:142
  1.0 0.1 copy.47
  1.1 0.1 slice_bitcast_fusion.3
  1.2 0.0 copy-start.4
  1.2 1.7 %slice_bitcast_fusion.1 = (bf16[24,4,32,64]{3,2,1,0:T(8,128)(2,1)S(1)}, bf16[24,4,32,64]{3,2,1,0:T(8,128)(2,1)S(1)}) fusion(bf16[24,2,4,32,64]{4,3,2,1,0:T(8,128)(2,1)} %param.15), kind=kLoop, calls=%fused_computation.11 | loop fusion | bytes 1572864 | tf_op jit(solution)/shard_map/squeeze | solution.py:143
  2.8 0.0 copy-start.5
  2.8 0.0 copy-done
  2.9 0.2 reshape.99
  3.0 0.1 copy.36
  3.1 0.1 iota_compare_fusion.3
  3.2 0.0 copy-done.4
  3.2 0.1 iota_compare_fusion.2
  3.3 0.1 pad_add_fusion
  3.4 0.7 %fusion.20 = (f32[24,4,8]{2,1,0:T(4,128)S(1)}, f32[24,4,8,34]{3,2,1,0:T(8,128)S(1)}) fusion(bf16[24,4,8,64]{3,2,1,0:T(8,128)(2,1)S(1)} %bitcast.51, bf16[24,4,2,64]{3,2,1,0:T(2,128)(2,1)S(1)} %get-tuple-element.7, bf16[24,4,32,64]{3,2,1,0:T(8,128)(2,1)S(1)} %get-tuple-element.5, pred[24,8,34]{2,1,0:T(8,128)(4,1)S(1)} %pad_add_fusion), kind=kOutput, calls=%fused_computation.46 | convolution fusion | flops 4255488 | bytes 630144 | tf_op jit(solution)/shard_map/rkgd,rkjd->rkgj/dot_general | solution.py:156
  4.1 0.0 copy-done.5
  4.1 0.1 tile.9
  4.2 0.1 tile.11
  4.3 0.4 fusion.8
  4.7 0.4 convolution_convert_fusion
  5.2 0.1 copy.46
  5.3 0.2 reshape.102
  5.4 0.0 copy-start.1
  5.5 0.0 copy-start.2
  5.5 0.0 copy-start.3
  5.5 5.4 %fusion.21.projected_ref = f32[48,2880]{1,0:T(8,128)} fusion(bf16[48,1024]{1,0:T(8,128)(2,1)S(1)} %reshape.102, bf16[1024,2880]{0,1:T(8,128)(2,1)} %param.18), kind=kOutput, calls=%fused_computation.47 | convolution fusion | flops 283115520 | bytes 6549504 | tf_op jit(solution)/shard_map/dot_general | solution.py:500
  10.9 0.0 copy-done.1
  10.9 0.6 broadcast_in_dim.34.gain_ref
  11.5 0.0 copy-done.2
  11.5 0.0 copy-done.3
  11.5 0.1 copy.39
  11.6 0.7 %fusion.17.pieces_ref = bf16[48,128]{1,0:T(8,128)(2,1)} fusion(bf16[48,8]{1,0:T(8,128)(2,1)S(1)} %get-tuple-element.10, bf16[48,8]{1,0:T(8,128)(2,1)S(1)} %get-tuple-element.11, bf16[48,8]{1,0:T(8,128)(2,1)S(1)} %get-tuple-element.9), kind=kLoop, calls=%fused_computation.37 | loop fusion | flops 61440 | bytes 14592 | tf_op jit(solution)/shard_map/concatenate | solution.py:508
  12.3 54.0 %shard_map.118 = bf16[48,1440]{1,0:T(8,128)(2,1)} custom-call(f32[48,2880]{1,0:T(8,128)} %fusion.21.projected_ref, bf16[48,1440]{1,0:T(8,128)(2,1)} %bitcast.64, bf16[1,2880]{1,0:T(2,128)(2,1)} %broadcast_in_dim.34.gain_ref, bf16[48,128]{1,0:T(8,128)(2,1)} %fusion.17.pieces_ref, bf16[2880,2,768]{2,1,0:T(2,128)(2,1)} %bitcast.62, bf16[2880,768]{1,0:T(8,128)(2,1)} %bitcast.63), custom_call_target="tpu_custom_call" | custom-call | flops 5096079360 | bytes 14680064 | tf_op jit(solution)/shard_map/pallas_call | solution.py:434
  66.3 1.6 %copy.49 = bf16[2,24,1440]{2,1,0:T(8,128)(2,1)} copy(bf16[2,24,1440]{2,1,0:T(8,128)(2,1)} %bitcast.58) | data formatting | bytes 276480
  (10 shorter events, 0.1 us)
Async XLA Ops:
  0.0 2.9 %copy-start = (bf16[2,24,1024]{2,1,0:T(8,128)(2,1)S(1)}, bf16[2,24,1024]{2,1,0:T(8,128)(2,1)}, u32[]{:S(2)}) copy-start(bf16[2,24,1024]{2,1,0:T(8,128)(2,1)} %param.13) | copy-start | bytes 294916
  1.2 2.0 %copy-start.4 = (s32[24]{0:T(128)S(1)}, s32[24]{0:T(128)}, u32[]{:S(2)}) copy-start(s32[24]{0:T(128)} %param.16) | copy-start | bytes 292
  2.8 1.3 %copy-start.5 = (f32[16]{0:T(128)S(1)}, f32[16]{0:T(128)}, u32[]{:S(2)}) copy-start(f32[16]{0:T(128)} %param.17) | copy-start | bytes 196
  5.4 5.4 %copy-start.1 = (bf16[2880]{0:T(1024)(128)(2,1)S(1)}, bf16[2880]{0:T(1024)(128)(2,1)}, u32[]{:S(2)}) copy-start(bf16[2880]{0:T(1024)(128)(2,1)} %param.19) | copy-start | bytes 17284
  5.5 6.0 %copy-start.2 = (f32[2,24,4]{1,2,0:T(4,128)S(1)}, f32[2,24,4]{1,2,0:T(4,128)}, u32[]{:S(2)}) copy-start(f32[2,24,4]{1,2,0:T(4,128)} %param.21) | copy-start | bytes 2308
  5.5 6.0 %copy-start.3 = (s32[2,24,4]{1,2,0:T(4,128)S(1)}, s32[2,24,4]{1,2,0:T(4,128)}, u32[]{:S(2)}) copy-start(s32[2,24,4]{1,2,0:T(4,128)} %param.20) | copy-start | bytes 2308
